TPU v7x, 256 devices: a whole 4x4x8 slice. The times are simulated.
256 devices in a mesh: span: 16 (over z, core), wall: 16 (over y, x).
Axes of the slice: x: 4, y: 4, z: 8, core: 2. Of those that a mesh axis runs over, the one named last changes fastest.
Arguments:
- residual: float32 [10, 10, 10, 32768], P(None, None, None, ('span', 'wall')), may hold values from -6 to 6
- eig_values: float32 [3, 12, 32768], P(None, None, ('span', 'wall')), may hold values from 0.1 to 20
- eig_vectors: float32 [3, 12, 12, 32768], P(None, None, None, ('span', 'wall')), may hold values from -1.75 to 1.75
- corner_map: int32 [8, 32768], P(None, ('span', 'wall')), may hold values from 0 to 4127, as said below
- stream_links: int32 [2, 16], replicated, may hold values from 0 to 15, as said below
- coarse_inverse: float32 [16, 4128, 4128], P('span', 'wall'), as said below
Outputs:
- preconditioned: float32 [10, 10, 10, 32768], P(None, None, None, ('span', 'wall'))
Inputs may be any that keep to these rules, and one draw needn't show every extreme that they name: `corner_map`: entry (c, e) names the coarse vertex at corner c = 4 a + 2 b + d of element e (a, b, d the upper or lower side along span, wall-normal and stream), numbered within the element's span slab; elements of one slab that share a corner name the same vertex, and every vertex of a slab is a corner of some element of it. `stream_links`: each row is a permutation of the slots; row 1 undoes row 0, and following row 1 from any slot visits all 16 slots before it returns. `coarse_inverse`: each slab's matrix is symmetric.
All inputs are finite; a program needn't handle non-finite values.
Results may differ from a plain program's by a relative error of at most 0.000067.
Values sent between devices are 32-bit elements; how exact they have to be, the bound alone decides.
A program may use at most 64 MiB of HBM per device.

v0:
```python
import jax
import jax.numpy as jnp
from jax import lax
from jax.sharding import PartitionSpec as P

PTS = 10
EXT = 12
EX = 1
EY = 8
EZ = 16


precise = lax.Precision.HIGHEST


def padded(array, sides, width, wrap):
    for axis, dim in sides:
        devices, length = (lax.axis_size(axis), array.shape[dim])
        up = [(i, (i + 1) % devices) for i in range(devices if wrap else devices - 1)]
        down = [(j, i) for i, j in up]
        last = lax.slice_in_dim(array, length - width, length, axis=dim)
        first = lax.slice_in_dim(array, 0, width, axis=dim)
        before = lax.ppermute(last, axis, up)
        after = lax.ppermute(first, axis, down)
        array = jnp.concatenate([before, array, after], axis=dim)
    return array


def corner_table(points):
    spots = (2.0 * jnp.arange(points, dtype=jnp.float32) + 1.0) / points - 1.0
    return jnp.stack([(1.0 - spots) * 0.5, (1.0 + spots) * 0.5])


def along_direction(matrix, field, along, forward):
    count = matrix.shape[0]
    batch = field.shape[-1]
    total = None
    for index in range(count):
        piece = lax.index_in_dim(field, index, along, keepdims=True)
        if forward:
            coeff = matrix[index]
        else:
            coeff = matrix[:, index]
        shaped = [1, 1, 1, batch]
        shaped[along] = count
        term = coeff.reshape(tuple(shaped)) * piece
        total = term if total is None else total + term
    return total


def fast_solve(extended, eig_values, eig_vectors):
    moved = along_direction(eig_vectors[0], extended, 0, True)
    moved = along_direction(eig_vectors[1], moved, 1, True)
    moved = along_direction(eig_vectors[2], moved, 2, True)
    divisor = (
        eig_values[0][:, None, None, :]
        + eig_values[1][None, :, None, :]
        + eig_values[2][None, None, :, :]
    )
    moved = moved / divisor
    moved = along_direction(eig_vectors[0], moved, 0, False)
    moved = along_direction(eig_vectors[1], moved, 1, False)
    return along_direction(eig_vectors[2], moved, 2, False)


def rims(span_pair, wall_pair):
    spanned = padded(span_pair, (("span", 0),), 1, True)
    walled = padded(wall_pair, (("wall", 0),), 1, False)
    lower_span = spanned[0]
    upper_span = spanned[3]
    lower_wall = walled[0]
    upper_wall = walled[3]
    return (lower_span, upper_span, lower_wall, upper_wall)


def coarse_total(vector):
    return lax.psum(vector, "wall")


def per_device(residual, eig_values, eig_vectors, corner_map, stream_links, coarse_inverse):
    elements = EX * EY * EZ
    columns = EY * EZ
    upstream = stream_links[0]
    downstream = stream_links[1]
    by_span = residual.reshape(PTS, PTS, PTS, EX, columns)
    by_grid = residual.reshape(PTS, PTS, PTS, EX, EY, EZ)
    span_pair = jnp.stack([by_span[0, :, :, 0], by_span[PTS - 1, :, :, EX - 1]]).reshape(2, -1)
    wall_pair = jnp.stack([by_grid[:, 0, :, :, 0], by_grid[:, PTS - 1, :, :, EY - 1]]).reshape(
        2, -1
    )
    lower_span, upper_span, lower_wall, upper_wall = rims(span_pair, wall_pair)
    face_xlow = jnp.concatenate(
        [lower_span.reshape(PTS, PTS, 1, columns), by_span[PTS - 1, :, :, : EX - 1]], axis=2
    )
    face_xhigh = jnp.concatenate(
        [by_span[0, :, :, 1:], upper_span.reshape(PTS, PTS, 1, columns)], axis=2
    )
    face_ylow = jnp.concatenate(
        [lower_wall.reshape(PTS, PTS, EX, 1, EZ), by_grid[:, PTS - 1, :, :, : EY - 1]], axis=3
    )
    face_yhigh = jnp.concatenate(
        [by_grid[:, 0, :, :, 1:], upper_wall.reshape(PTS, PTS, EX, 1, EZ)], axis=3
    )
    face_zlow = jnp.take(by_grid[:, :, PTS - 1], upstream, axis=4)
    face_zhigh = jnp.take(by_grid[:, :, 0], downstream, axis=4)
    extended = jnp.zeros((EXT, EXT, EXT, elements), jnp.float32)
    extended = extended.at[1:-1, 1:-1, 1:-1].set(residual)
    extended = extended.at[0, 1:-1, 1:-1].set(face_xlow.reshape(PTS, PTS, elements))
    extended = extended.at[EXT - 1, 1:-1, 1:-1].set(face_xhigh.reshape(PTS, PTS, elements))
    extended = extended.at[1:-1, 0, 1:-1].set(face_ylow.reshape(PTS, PTS, elements))
    extended = extended.at[1:-1, EXT - 1, 1:-1].set(face_yhigh.reshape(PTS, PTS, elements))
    extended = extended.at[1:-1, 1:-1, 0].set(face_zlow.reshape(PTS, PTS, elements))
    extended = extended.at[1:-1, 1:-1, EXT - 1].set(face_zhigh.reshape(PTS, PTS, elements))
    solved = fast_solve(extended, eig_values, eig_vectors)
    solved_x0 = solved[0, 1:-1, 1:-1].reshape(PTS, PTS, EX, columns)
    solved_x1 = solved[EXT - 1, 1:-1, 1:-1].reshape(PTS, PTS, EX, columns)
    solved_y0 = solved[1:-1, 0, 1:-1].reshape(PTS, PTS, EX, EY, EZ)
    solved_y1 = solved[1:-1, EXT - 1, 1:-1].reshape(PTS, PTS, EX, EY, EZ)
    solved_z0 = solved[1:-1, 1:-1, 0].reshape(PTS, PTS, EX, EY, EZ)
    solved_z1 = solved[1:-1, 1:-1, EXT - 1].reshape(PTS, PTS, EX, EY, EZ)
    span_back = jnp.stack([solved_x0[:, :, 0], solved_x1[:, :, EX - 1]]).reshape(2, -1)
    wall_back = jnp.stack([solved_y0[:, :, :, 0], solved_y1[:, :, :, EY - 1]]).reshape(2, -1)
    back_lspan, back_uspan, back_lwall, back_uwall = rims(span_back, wall_back)
    add_xlow = jnp.concatenate(
        [back_lspan.reshape(PTS, PTS, 1, columns), solved_x1[:, :, : EX - 1]], axis=2
    )
    add_xhigh = jnp.concatenate(
        [solved_x0[:, :, 1:], back_uspan.reshape(PTS, PTS, 1, columns)], axis=2
    )
    add_ylow = jnp.concatenate(
        [back_lwall.reshape(PTS, PTS, EX, 1, EZ), solved_y1[:, :, :, : EY - 1]], axis=3
    )
    add_yhigh = jnp.concatenate(
        [solved_y0[:, :, :, 1:], back_uwall.reshape(PTS, PTS, EX, 1, EZ)], axis=3
    )
    add_zlow = jnp.take(solved_z1, upstream, axis=4)
    add_zhigh = jnp.take(solved_z0, downstream, axis=4)
    inner = solved[1:-1, 1:-1, 1:-1]
    inner = inner.at[0].add(add_xlow.reshape(PTS, PTS, elements))
    inner = inner.at[PTS - 1].add(add_xhigh.reshape(PTS, PTS, elements))
    inner = inner.at[:, 0].add(add_ylow.reshape(PTS, PTS, elements))
    inner = inner.at[:, PTS - 1].add(add_yhigh.reshape(PTS, PTS, elements))
    inner = inner.at[:, :, 0].add(add_zlow.reshape(PTS, PTS, elements))
    inner = inner.at[:, :, PTS - 1].add(add_zhigh.reshape(PTS, PTS, elements))
    table = corner_table(PTS)
    corner_sums = jnp.einsum(
        "at,bu,dv,tuve->abde", table, table, table, residual, precision=precise
    ).reshape(8, elements)
    vertices = coarse_inverse.shape[2]
    partial_value = jax.ops.segment_sum(
        corner_sums.reshape(-1), corner_map.reshape(-1), num_segments=vertices
    )
    row_block = coarse_inverse[0]
    summed = coarse_total(partial_value)
    own_rows = jnp.dot(row_block, summed, precision=precise)
    coarse_sol = lax.all_gather(own_rows, "wall", axis=0, tiled=True)
    at_corners = coarse_sol[corner_map].reshape(2, 2, 2, elements)
    lifted = jnp.einsum("at,bu,dv,abde->tuve", table, table, table, at_corners, precision=precise)
    return inner + lifted


def solution(mesh):
    return jax.shard_map(
        per_device,
        mesh=mesh,
        in_specs=(
            P(None, None, None, ("span", "wall")),
            P(None, None, ("span", "wall")),
            P(None, None, None, ("span", "wall")),
            P(None, ("span", "wall")),
            P(),
            P("span", "wall", None),
        ),
        out_specs=P(None, None, None, ("span", "wall")),
        check_vma=False,
    )
```

profile of v0, /device:TPU:8, one launch (start us, length us, event | category | flops | bytes accessed | tf_op | source)
XLA Modules:
  0.0 259.4 jit_solution(10939363533648223000)
XLA Ops:
  2.3 5.3 %collective-permute-start.1 = (f32[1,12800]{1,0:T(1,128)}, f32[1,12800]{1,0:T(1,128)S(1)}, u32[]{:S(2)}, u32[]{:S(2)}) collective-permute-start(f32[1,12800]{1,0:T(1,128)} %slice.1051), channel_id=1, source_target_pairs={{16,0},{32,16},{48,32},{64,48},{80,64},{96,80},{112,96},{128,112},... | collective-permute-start | bytes 153608 | tf_op jit(solution)/shard_map/ppermute | solution.py:24
  7.6 3.8 %reshape.709 = f32[10,10,10,1,8,16]{5,4,2,1,0,3:T(8,128)} reshape(f32[10,10,10,128]{3,2,1,0:T(8,128)} %param.34) | data formatting | bytes 1024000 | tf_op jit(solution)/shard_map/reshape | solution.py:86
  11.4 1.4 slice_reduce_fusion.4
  13.5 3.4 %collective-permute-start.2 = (f32[1,1600]{1,0:T(1,128)}, f32[1,1600]{1,0:T(1,128)}, u32[]{:S(2)}, u32[]{:S(2)}) collective-permute-start(f32[1,1600]{1,0:T(1,128)} %slice.1053), channel_id=1, source_target_pairs={{0,1},{1,2},{2,3},{3,4},{4,5},{5,6},{6,7},{7,8},{8,9},{9,10},{10,1... | collective-permute-start | bytes 19208 | tf_op jit(solution)/shard_map/ppermute | solution.py:23
  17.5 4.5 %collective-permute-start.3 = (f32[1,1600]{1,0:T(1,128)}, f32[1,1600]{1,0:T(1,128)}, u32[]{:S(2)}, u32[]{:S(2)}) collective-permute-start(f32[1,1600]{1,0:T(1,128)} %slice.1057), channel_id=1, source_target_pairs={{1,0},{2,1},{3,2},{4,3},{5,4},{6,5},{7,6},{8,7},{9,8},{10,9},{11,1... | collective-permute-start | bytes 19208 | tf_op jit(solution)/shard_map/ppermute | solution.py:24
  22.1 2.1 fusion.27
  31.9 5.9 %scatter_custom_fusion = f32[4128]{0:T(1024)S(1)} fusion(s32[1024]{0:T(1024)S(1)} %bitcast.465, f32[1024]{0:T(1024)S(1)} %bitcast.464, f32[]{:T(128)} %constant.404.clone.1), kind=kCustom, calls=%fused_computation.128 | custom fusion | flops 1024 | bytes 16516 | tf_op jit(solution)/shard_map/scatter-add | solution.py:150
  37.8 66.9 %psum.7 = f32[4128]{0:T(1024)S(1)} all-reduce(f32[4128]{0:T(1024)S(1)} %scatter_custom_fusion), channel_id=1, replica_groups=mesh['span'=16,'wall'=16] {'wall'}, use_global_device_ids=true, to_apply=%region_1.3 | all-reduce | flops 4128 | bytes 33024 | tf_op jit(solution)/shard_map/psum | solution.py:77
  104.8 6.2 %fusion.4 = f32[258]{0:T(512)S(1)} fusion(f32[4128,1]{0,1:T(1,128)S(1)} %reshape.807, f32[1,258,4128]{2,0,1:T(1,128)} %param.39), kind=kOutput, calls=%fused_computation.18 | convolution fusion | flops 12780288 | bytes 4277640 | tf_op jit(solution)/shard_map/dot_general | solution.py:155
  112.4 69.7 %all-reduce.1 = f32[4128]{0:T(1024)S(1)} all-reduce(f32[4128]{0:T(1024)S(1)} %dynamic-update-slice.39), channel_id=1, replica_groups=mesh['span'=16,'wall'=16] {'wall'}, use_global_device_ids=true, to_apply=%add.1 | all-reduce | flops 4128 | bytes 33024
  182.1 6.1 %gather_fusion = f32[1024]{0:T(1024)S(1)} fusion(f32[4128]{0:T(1024)S(1)} %all-reduce.1, s32[1024]{0:T(1024)S(1)} %fusion.22), kind=kCustom, calls=%fused_computation.4 | custom fusion | bytes 12288 | tf_op jit(solution)/shard_map/gather | solution.py:157
  206.9 1.6 scatter.31
  208.5 1.8 scatter.34
  221.9 3.0 %collective-permute-start.5 = (f32[1,12800]{1,0:T(1,128)}, f32[1,12800]{1,0:T(1,128)}, u32[]{:S(2)}, u32[]{:S(2)}) collective-permute-start(f32[1,12800]{1,0:T(1,128)} %slice.1209), channel_id=1, source_target_pairs={{16,0},{32,16},{48,32},{64,48},{80,64},{96,80},{112,96},{128,112},... | collective-permute-start | bytes 153608 | tf_op jit(solution)/shard_map/ppermute | solution.py:24
  225.8 1.9 collective-permute-start.6
  228.4 6.0 %collective-permute-start.7 = (f32[1,1600]{1,0:T(1,128)}, f32[1,1600]{1,0:T(1,128)}, u32[]{:S(2)}, u32[]{:S(2)}) collective-permute-start(f32[1,1600]{1,0:T(1,128)} %slice.1219), channel_id=1, source_target_pairs={{1,0},{2,1},{3,2},{4,3},{5,4},{6,5},{7,6},{8,7},{9,8},{10,9},{11,1... | collective-permute-start | bytes 19208 | tf_op jit(solution)/shard_map/ppermute | solution.py:24
  235.2 1.6 gather_fusion.4
  237.5 1.6 gather_fusion.3
  239.1 1.4 bitcast_select_fusion
  243.2 1.3 copy.49
  244.5 1.8 reshape.719
  252.1 2.7 %scatter-add.34 = f32[10,10,10,128]{3,2,1,0:T(8,128)S(1)} dynamic-update-slice(f32[10,10,10,128]{3,2,1,0:T(8,128)S(1)} %fusion.11, f32[10,10,1,128]{3,2,1,0:T(1,128)S(1)} %slice_add_fusion.5, s32[]{:T(128)} %constant.405.clone.1, s32[]{:T(128)} %constant.405.clone.1, s32[]{:T(128)} %constant.405.clone.1, s32[]{:T(128)} %constant.405.clone.1) | dynamic-update-slice | bytes 102404 | tf_op jit(solution)/shard_map/scatter-add | solution.py:143
  254.9 2.7 %scatter-add.42 = f32[10,10,10,128]{3,2,1,0:T(8,128)S(1)} dynamic-update-slice(f32[10,10,10,128]{3,2,1,0:T(8,128)S(1)} %scatter-add.34, f32[10,10,1,128]{3,2,1,0:T(1,128)S(1)} %slice_add_fusion.4, s32[]{:T(128)} %constant.405.clone.1, s32[]{:T(128)} %constant.405.clone.1, s32[]{:T(128)} %constant.408.clone.1, s32[]{:T(128)} %constant.405.clone.1) | dynamic-update-slice | bytes 102404 | tf_op jit(solution)/shard_map/scatter-add | solution.py:144
  257.6 1.7 fusion.3
  (320 shorter events, 52.4 us)
Async XLA Ops:
  1.6 204.2 %collective-permute-start = (f32[1,12800]{1,0:T(1,128)}, f32[1,12800]{1,0:T(1,128)S(1)}, u32[]{:S(2)}, u32[]{:S(2)}) collective-permute-start(f32[1,12800]{1,0:T(1,128)} %slice.1049), channel_id=1, source_target_pairs={{0,16},{16,32},{32,48},{48,64},{64,80},{80,96},{96,112},{112,128},... | collective-permute-start | bytes 153608 | tf_op jit(solution)/shard_map/ppermute | solution.py:23
  2.3 203.7 %collective-permute-start.1 = (f32[1,12800]{1,0:T(1,128)}, f32[1,12800]{1,0:T(1,128)S(1)}, u32[]{:S(2)}, u32[]{:S(2)}) collective-permute-start(f32[1,12800]{1,0:T(1,128)} %slice.1051), channel_id=1, source_target_pairs={{16,0},{32,16},{48,32},{64,48},{80,64},{96,80},{112,96},{128,112},... | collective-permute-start | bytes 153608 | tf_op jit(solution)/shard_map/ppermute | solution.py:24
  13.5 187.8 %collective-permute-start.2 = (f32[1,1600]{1,0:T(1,128)}, f32[1,1600]{1,0:T(1,128)}, u32[]{:S(2)}, u32[]{:S(2)}) collective-permute-start(f32[1,1600]{1,0:T(1,128)} %slice.1053), channel_id=1, source_target_pairs={{0,1},{1,2},{2,3},{3,4},{4,5},{5,6},{6,7},{7,8},{8,9},{9,10},{10,1... | collective-permute-start | bytes 19208 | tf_op jit(solution)/shard_map/ppermute | solution.py:23
  17.5 186.0 %collective-permute-start.3 = (f32[1,1600]{1,0:T(1,128)}, f32[1,1600]{1,0:T(1,128)}, u32[]{:S(2)}, u32[]{:S(2)}) collective-permute-start(f32[1,1600]{1,0:T(1,128)} %slice.1057), channel_id=1, source_target_pairs={{1,0},{2,1},{3,2},{4,3},{5,4},{6,5},{7,6},{8,7},{9,8},{10,9},{11,1... | collective-permute-start | bytes 19208 | tf_op jit(solution)/shard_map/ppermute | solution.py:24
  26.8 161.7 %copy-start.71 = (f32[1,10]{1,0:T(1,128)}, f32[1,10]{1,0:T(1,128)S(1)}, u32[]{:S(2)}) copy-start(f32[1,10]{1,0:T(1,128)S(1)} %get-tuple-element.334) | copy-start | bytes 124
  26.8 161.7 %copy-start.73 = (f32[1,10]{1,0:T(1,128)}, f32[1,10]{1,0:T(1,128)S(1)}, u32[]{:S(2)}) copy-start(f32[1,10]{1,0:T(1,128)S(1)} %get-tuple-element.335) | copy-start | bytes 124
  28.0 162.1 %copy-start.79 = (pred[16]{0:T(512)(128)(4,1)}, pred[16]{0:T(512)(128)(4,1)S(1)}, u32[]{:S(2)}) copy-start(pred[16]{0:T(512)(128)(4,1)S(1)} %get-tuple-element.330) | copy-start | bytes 52
  28.1 162.9 %copy-start.77 = (pred[16]{0:T(512)(128)(4,1)}, pred[16]{0:T(512)(128)(4,1)S(1)}, u32[]{:S(2)}) copy-start(pred[16]{0:T(512)(128)(4,1)S(1)} %get-tuple-element.166) | copy-start | bytes 52
  28.1 161.5 %copy-start.75 = (s32[1024]{0:T(1024)}, s32[1024]{0:T(1024)S(1)}, u32[]{:S(2)}) copy-start(s32[1024]{0:T(1024)S(1)} %pad_clamp_fusion.1) | copy-start | bytes 12292
  28.7 161.7 %copy-start.76 = (s32[1024]{0:T(1024)}, s32[1024]{0:T(1024)S(1)}, u32[]{:S(2)}) copy-start(s32[1024]{0:T(1024)S(1)} %pad_clamp_fusion) | copy-start | bytes 12292
  194.1 7.0 %copy-start.46 = (f32[12,1,128]{2,1,0:T(1,128)S(1)}, f32[12,1,128]{2,1,0:T(1,128)}, u32[]{:S(2)}) copy-start(f32[12,1,128]{2,1,0:T(1,128)} %get-tuple-element.299) | copy-start | bytes 18436
  194.1 7.0 %copy-start.45 = (f32[12,1,128]{2,1,0:T(1,128)S(1)}, f32[12,1,128]{2,1,0:T(1,128)}, u32[]{:S(2)}) copy-start(f32[12,1,128]{2,1,0:T(1,128)} %get-tuple-element.300) | copy-start | bytes 18436
  194.1 7.0 %copy-start.44 = (f32[12,1,128]{2,1,0:T(1,128)S(1)}, f32[12,1,128]{2,1,0:T(1,128)}, u32[]{:S(2)}) copy-start(f32[12,1,128]{2,1,0:T(1,128)} %get-tuple-element.301) | copy-start | bytes 18436
  194.1 7.1 %copy-start.43 = (f32[12,1,128]{2,1,0:T(1,128)S(1)}, f32[12,1,128]{2,1,0:T(1,128)}, u32[]{:S(2)}) copy-start(f32[12,1,128]{2,1,0:T(1,128)} %get-tuple-element.302) | copy-start | bytes 18436
  194.1 7.1 %copy-start.42 = (f32[12,1,128]{2,1,0:T(1,128)S(1)}, f32[12,1,128]{2,1,0:T(1,128)}, u32[]{:S(2)}) copy-start(f32[12,1,128]{2,1,0:T(1,128)} %get-tuple-element.291) | copy-start | bytes 18436
  194.4 7.7 %copy-start.6 = (f32[10,10,1,7,16]{4,2,3,1,0:T(1,128)S(1)}, f32[10,10,1,7,16]{4,2,3,1,0:T(1,128)}, u32[]{:S(2)}) copy-start(f32[10,10,1,7,16]{4,2,3,1,0:T(1,128)} %squeeze.36) | copy-start | bytes 134404
  221.2 28.8 %collective-permute-start.4 = (f32[1,12800]{1,0:T(1,128)}, f32[1,12800]{1,0:T(1,128)}, u32[]{:S(2)}, u32[]{:S(2)}) collective-permute-start(f32[1,12800]{1,0:T(1,128)} %slice.1206), channel_id=1, source_target_pairs={{0,16},{16,32},{32,48},{48,64},{64,80},{80,96},{96,112},{112,128},... | collective-permute-start | bytes 153608 | tf_op jit(solution)/shard_map/ppermute | solution.py:23
  221.9 29.1 %collective-permute-start.5 = (f32[1,12800]{1,0:T(1,128)}, f32[1,12800]{1,0:T(1,128)}, u32[]{:S(2)}, u32[]{:S(2)}) collective-permute-start(f32[1,12800]{1,0:T(1,128)} %slice.1209), channel_id=1, source_target_pairs={{16,0},{32,16},{48,32},{64,48},{80,64},{96,80},{112,96},{128,112},... | collective-permute-start | bytes 153608 | tf_op jit(solution)/shard_map/ppermute | solution.py:24
  225.0 11.8 %copy-start.1 = (f32[10,10,1,8,16]{4,3,2,1,0:T(8,128)}, f32[10,10,1,8,16]{4,3,2,1,0:T(8,128)S(1)}, u32[]{:S(2)}) copy-start(f32[10,10,1,8,16]{4,3,2,1,0:T(8,128)S(1)} %reshape_squeeze.18) | copy-start | bytes 153604
  225.8 20.4 %collective-permute-start.6 = (f32[1,1600]{1,0:T(1,128)}, f32[1,1600]{1,0:T(1,128)}, u32[]{:S(2)}, u32[]{:S(2)}) collective-permute-start(f32[1,1600]{1,0:T(1,128)} %slice.1213), channel_id=1, source_target_pairs={{0,1},{1,2},{2,3},{3,4},{4,5},{5,6},{6,7},{7,8},{8,9},{9,10},{10,1... | collective-permute-start | bytes 19208 | tf_op jit(solution)/shard_map/ppermute | solution.py:23
  228.4 18.7 %collective-permute-start.7 = (f32[1,1600]{1,0:T(1,128)}, f32[1,1600]{1,0:T(1,128)}, u32[]{:S(2)}, u32[]{:S(2)}) collective-permute-start(f32[1,1600]{1,0:T(1,128)} %slice.1219), channel_id=1, source_target_pairs={{1,0},{2,1},{3,2},{4,3},{5,4},{6,5},{7,6},{8,7},{9,8},{10,9},{11,1... | collective-permute-start | bytes 19208 | tf_op jit(solution)/shard_map/ppermute | solution.py:24
  249.8 7.8 %copy-start.8 = (f32[2,128,10,10]{1,3,2,0:T(8,128)S(1)}, f32[2,128,10,10]{1,3,2,0:T(8,128)}, u32[]{:S(2)}) copy-start(f32[2,128,10,10]{1,3,2,0:T(8,128)} %fusion.17) | copy-start | bytes 307204
  249.8 7.8 %copy-start.72 = (f32[1,10]{1,0:T(1,128)S(1)}, f32[1,10]{1,0:T(1,128)}, u32[]{:S(2)}) copy-start(f32[1,10]{1,0:T(1,128)} %copy-done.71) | copy-start | bytes 124
  249.8 7.8 %copy-start.74 = (f32[1,10]{1,0:T(1,128)S(1)}, f32[1,10]{1,0:T(1,128)}, u32[]{:S(2)}) copy-start(f32[1,10]{1,0:T(1,128)} %copy-done.73) | copy-start | bytes 124
  (68 other events, 226.6 us)
where the time goes:
time: 263 us; the launch traced here: 259 us
  blocking collectives  137 us (52%)
  local copies, waits for them, and re-layouts  63.7 us (24%)
  starting transfers between devices  24.1 us (9%)
  other arithmetic  22.2 us (8%)
  matrix products  10.3 us (4%)
    unnamed x1, blocking collectives  69.7 us
    psum x1, blocking collectives, coarse_total(): return lax.psum(vector, 'wall')  66.9 us
    ppermute x4, starting transfers between devices, padded(): after = lax.ppermute(first, axis, down)  18.8 us
    unnamed x209, local copies, waits for them, and re-layouts  10.7 us
    dot_general x1, matrix products, per_device(): own_rows = jnp.dot(row_block, summed, precision=precise)  6.15 us
    gather x1, local copies, waits for them, and re-layouts, per_device(): at_corners = coarse_sol[corner_map].reshape(2, 2, 2, elements)  6.14 us
    scatter-add x1, other arithmetic, per_device(): jax.ops.segment_sum(corner_sums.reshape(-1), corner_map.reshape(-1), num_...  5.93 us
    ppermute x4, starting transfers between devices, padded(): before = lax.ppermute(last, axis, up)  5.3 us
  transfers between devices with their start and end apart: 8, of which 0 were waited for; matrix products, arithmetic and copies ran while one was open for 27% of the time, Pallas kernels for 0%

commit v1 on v0

v1 whole, which is shorter than its diff:
```python
import functools

import jax
import jax.numpy as jnp
from jax import lax
from jax.experimental import pallas as pl
from jax.experimental.pallas import tpu as pltpu
from jax.sharding import PartitionSpec as P

PTS = 10
EXT = 12
EY = 8
EZ = 16
LANES = 128
SLAB = EXT * EXT
GROUP = 2 * EXT
POINT = tuple(range(1, PTS + 1)) + (0, EXT - 1)
LOW, HIGH = PTS, PTS + 1
precise = lax.Precision.HIGHEST
f32 = jnp.float32


def upper(index):
    return (2 * index + 1) / (2 * PTS)


def rows_of(shape):
    return lax.broadcasted_iota(jnp.int32, shape, 0)


def lanes_of(shape):
    return lax.broadcasted_iota(jnp.int32, shape, 1)


def turn(values, shift):
    return pltpu.roll(values, shift % LANES, 1)


def permute(values, index):
    return jnp.take_along_axis(values, jnp.broadcast_to(index, values.shape), axis=1)


def divider(rows, top):
    for shift in range(12, 26):
        factor = -(-(1 << shift) // rows)
        if top * factor < 1 << 31 and all((v * factor) >> shift == v // rows for v in range(top)):
            return factor, shift
    raise ValueError("no divider")


def contract(count, groups, first, load, coeff, store):
    def body(group, carry):
        pieces = load(group)
        for o in range(EXT):
            total = None
            for i in range(count):
                term = coeff(o, i) * pieces[i]
                total = term if total is None else total + term
            store(group, o, total)
        return carry

    lax.fori_loop(first, groups, body, 0)


def kernel(
    spans, walls, verts,
    res_in, val_in, vec_in, map_in, link_in, inv_in, out,
    field, faces, ping, pong, solved, vec, val, cmap, links, inv,
    acc, csum, xown, xall, yown, yall, pack_out, pack_in, face_in,
    local_sem, out_sem, span_send, span_recv, wall_send, wall_recv, x_send, x_recv, y_send, y_recv,
):
    s = lax.axis_index("span")
    w = lax.axis_index("wall")
    rows = verts // walls
    tiles = verts // LANES
    rest = verts - tiles * LANES
    inner = pl.ds(0, PTS)

    load_field = pltpu.make_async_copy(res_in, field.at[inner, inner, inner, :], local_sem.at[0])
    load_map = pltpu.make_async_copy(map_in, cmap, local_sem.at[1])
    load_links = pltpu.make_async_copy(link_in, links, local_sem.at[2])
    load_vec = pltpu.make_async_copy(vec_in, vec, local_sem.at[3])
    load_val = pltpu.make_async_copy(val_in, val, local_sem.at[4])
    load_inv = pltpu.make_async_copy(inv_in.at[0], inv, local_sem.at[5])
    for copy in (load_field, load_map, load_links, load_vec, load_val, load_inv):
        copy.start()

    barrier = pltpu.get_barrier_semaphore()
    for k in range(1, walls):
        pl.semaphore_signal(barrier, inc=1, device_id={"wall": lax.rem(w + k, walls)})
    above = lax.rem(s + 1, spans)
    below = lax.rem(s + spans - 1, spans)
    for peer in (above, below):
        pl.semaphore_signal(barrier, inc=1, device_id={"span": peer})
    pl.semaphore_wait(barrier, walls + 1)

    def remote(src, dst, send, recv, axis, peer):
        return pltpu.make_async_remote_copy(
            src_ref=src, dst_ref=dst, send_sem=send, recv_sem=recv, device_id={axis: peer}
        )

    span_first = [
        remote(res_in.at[PTS - 1], faces.at[0, inner, inner, :], span_send.at[0], span_recv.at[0], "span", above),
        remote(res_in.at[0], faces.at[1, inner, inner, :], span_send.at[1], span_recv.at[1], "span", below),
    ]
    for copy in span_first:
        copy.start()

    def wall_copies(turn_index):
        base = 2 * turn_index
        up = remote(pack_out.at[base], pack_in.at[base], wall_send.at[base], wall_recv.at[base],
                    "wall", lax.rem(w + 1, walls))
        down = remote(pack_out.at[base + 1], pack_in.at[base + 1], wall_send.at[base + 1], wall_recv.at[base + 1],
                      "wall", lax.rem(w + walls - 1, walls))
        return up, down

    has_up = w < walls - 1
    has_down = w > 0

    def send_walls(turn_index):
        up, down = wall_copies(turn_index)
        pl.when(has_up)(up.start)
        pl.when(has_down)(down.start)

    def receive_walls(turn_index):
        up, down = wall_copies(turn_index)
        pl.when(has_down)(up.wait_recv)
        pl.when(has_up)(down.wait_recv)

    def finish_walls(turn_index):
        up, down = wall_copies(turn_index)
        pl.when(has_up)(up.wait_send)
        pl.when(has_down)(down.wait_send)

    lane = lanes_of((8, LANES))
    slot_of = lane // EZ

    def pack(source, layer, lane_from, dest):
        parts = [None] * 3
        for t in range(PTS):
            for half in range(2):
                slot = 2 * t + half
                piece = source[t, layer, pl.ds(8 * half, 8), :]
                place = slot % 8
                moved = turn(piece, EZ * place - lane_from)
                held = parts[slot // 8]
                parts[slot // 8] = moved if held is None else jnp.where(slot_of == place, moved, held)
        for index, part in enumerate(parts):
            pack_out[dest, pl.ds(8 * index, 8), :] = part

    def unpack(buffer, t, half, lane_to):
        slot = 2 * t + half
        part = pack_in[buffer, pl.ds(8 * (slot // 8), 8), :]
        return turn(part, lane_to - EZ * (slot % 8))

    @pl.when(jnp.logical_not(has_down))
    def _():
        for turn_index in range(2):
            pack_in[2 * turn_index] = jnp.zeros(pack_in.shape[1:], f32)

    @pl.when(jnp.logical_not(has_up))
    def _():
        for turn_index in range(2):
            pack_in[2 * turn_index + 1] = jnp.zeros(pack_in.shape[1:], f32)

    blank = jnp.zeros((16 - PTS, LANES), f32)
    for t in range(PTS):
        field[t, 0, pl.ds(PTS, 16 - PTS), :] = blank
        field[t, PTS - 1, pl.ds(PTS, 16 - PTS), :] = blank
    for side in range(2):
        for u in (LOW, HIGH):
            faces[side, u] = jnp.zeros((16, LANES), f32)
    csum[...] = jnp.zeros(csum.shape, f32)
    acc[...] = jnp.zeros(acc.shape, f32)

    load_links.wait()
    lane_row = lanes_of((8, LANES))
    place = lane_row % EZ
    up_slot = jnp.zeros((8, LANES), jnp.int32)
    down_slot = jnp.zeros((8, LANES), jnp.int32)
    for q in range(EZ):
        up_slot = jnp.where(place == q, links[0, q], up_slot)
        down_slot = jnp.where(place == q, links[1, q], down_slot)
    line = lane_row - place
    upstream8 = line + up_slot
    downstream8 = line + down_slot
    upstream = jnp.concatenate([upstream8] * 3, axis=0)
    downstream = jnp.concatenate([downstream8] * 3, axis=0)

    load_field.wait()
    pack(field, PTS - 1, LANES - EZ, 0)
    pack(field, 0, 0, 1)
    send_walls(0)

    def corner_body(u, sums):
        total = None
        weighted = None
        for t in range(PTS):
            piece = field[t, u, inner, :]
            term = piece * upper(t)
            total = piece if total is None else total + piece
            weighted = term if weighted is None else weighted + term
        low = total - weighted
        share = (2.0 * u.astype(f32) + 1.0) / (2 * PTS)
        low_up = low * share
        high_up = weighted * share
        return (sums[0] + (low - low_up), sums[1] + low_up,
                sums[2] + (weighted - high_up), sums[3] + high_up)

    nothing = jnp.zeros((PTS, LANES), f32)
    sums = lax.fori_loop(0, PTS, corner_body, (nothing,) * 4)
    share_v = (2.0 * rows_of((PTS, LANES)).astype(f32) + 1.0) / (2 * PTS)
    for ab in range(4):
        upper_part = sums[ab] * share_v
        csum[0, pl.ds(ab, 1), :] = jnp.sum(sums[ab] - upper_part, axis=0, keepdims=True)
        csum[1, pl.ds(ab, 1), :] = jnp.sum(upper_part, axis=0, keepdims=True)
    lines = csum[0] + permute(csum[1], upstream8)
    moved_up = jnp.where(lane >= EZ, turn(lines, EZ), 0.0)
    moved_down = turn(lines, -EZ)
    lane1 = lanes_of((1, LANES))
    last_line = lane1 >= LANES - EZ
    second_line = lane1 >= LANES - 2 * EZ
    values = jnp.concatenate([
        lines[0:1] + moved_up[1:2],
        lines[2:3] + moved_up[3:4],
        jnp.where(last_line, lines[1:2], jnp.where(second_line, moved_down[3:4], 0.0)),
    ], axis=1)

    load_map.wait()
    moved_map = turn(cmap[...], -EZ)
    ids = jnp.concatenate([
        cmap[0:1, :],
        cmap[4:5, :],
        jnp.where(last_line, cmap[2:3, :], jnp.where(second_line, moved_map[6:7], -1)),
    ], axis=1)
    width = 3 * LANES
    held = xown.shape[0]
    spread = jnp.where(rows_of((held, width)) == (ids >> 7), values, 0.0)
    onehot = (rows_of((LANES, width)) == (ids & (LANES - 1))).astype(f32)
    xown[...] = lax.dot_general(
        spread, onehot, (((1,), (1,)), ((), ())), precision=precise, preferred_element_type=f32
    )

    def x_copy(k):
        return remote(xown, xall.at[k], x_send.at[k], x_recv.at[k], "wall", lax.rem(w + k, walls))

    for k in range(1, walls):
        x_copy(k).start()

    receive_walls(0)
    first_line = lane < EZ
    end_line = lane >= LANES - EZ
    for t in range(PTS):
        for half in range(2):
            span_rows = pl.ds(8 * half, 8)
            low = turn(field[t, PTS - 1, span_rows, :], EZ)
            field[t, LOW, span_rows, :] = jnp.where(first_line, unpack(0, t, half, 0), low)
            high = turn(field[t, 0, span_rows, :], -EZ)
            field[t, HIGH, span_rows, :] = jnp.where(end_line, unpack(1, t, half, LANES - EZ), high)

    def vector(direction, point, mode):
        return jnp.broadcast_to(vec[direction, point, pl.ds(mode, 1), :], (GROUP, LANES))

    def strided(ref):
        return lambda g: [ref[pl.ds(g * (GROUP * EXT) + i, GROUP, stride=EXT), :] for i in range(EXT)]

    def dense(ref):
        def put(g, o, total):
            ref[pl.ds(pl.multiple_of(o * SLAB + g * GROUP, 8), GROUP), :] = total
        return put

    load_vec.wait()
    load_val.wait()
    flat_field = field.reshape(PTS * EXT * 16, LANES)
    flat_faces = faces.reshape(2 * EXT * 16, LANES)
    inside = (rows_of((GROUP, LANES)) % EXT) < PTS

    def load_first(g):
        pieces = [flat_field[pl.ds(g * (GROUP * 16) + v, GROUP, stride=16), :] for v in range(PTS)]
        pieces.append(jnp.where(inside, permute(pieces[PTS - 1], upstream), 0.0))
        pieces.append(jnp.where(inside, permute(pieces[0], downstream), 0.0))
        return pieces

    def load_faces(g):
        return [flat_faces[pl.ds(v, GROUP, stride=16), :] for v in range(PTS)]

    forward = lambda d: lambda o, i: vector(d, POINT[i], o)
    backward = lambda d: lambda o, i: vector(d, POINT[o], i)
    contract(EXT, PTS // 2, 0, load_first, forward(2), dense(ping))
    for copy in span_first:
        copy.wait_recv()
    contract(PTS, EXT // 2, PTS // 2, load_faces, forward(2), dense(ping))
    contract(EXT, EXT // 2, 0, strided(ping), forward(1), dense(pong))

    second_half = rows_of((GROUP, LANES)) >= EXT
    third = jnp.concatenate([val[2], val[2]], axis=0)

    def scaled(ref):
        put = dense(ref)

        def divide(g, o, total):
            firsts = jnp.broadcast_to(val[1, pl.ds(2 * g, 1), :], (GROUP, LANES))
            seconds = jnp.broadcast_to(val[1, pl.ds(2 * g + 1, 1), :], (GROUP, LANES))
            both = jnp.where(second_half, seconds, firsts) + third
            put(g, o, total / (jnp.broadcast_to(val[0, pl.ds(o, 1), :], (GROUP, LANES)) + both))
        return divide

    contract(EXT, EXT // 2, 0, strided(pong), forward(0), scaled(ping))

    load_inv.wait()
    for k in range(1, walls):
        x_copy(k).wait_recv()
    total_x = xown[...]
    for k in range(1, walls):
        total_x = total_x + xall[k]
    xall[0] = total_x

    def times(start, count):
        total = None
        for c in range(tiles):
            term = inv[pl.ds(start, count), pl.ds(c * LANES, LANES)] * xall[0, pl.ds(c, 1), :]
            total = term if total is None else total + term
        acc[0, pl.ds(start, count), :] = total
        if rest:
            tail = inv[pl.ds(start, count), pl.ds(tiles * LANES, rest)] * xall[0, pl.ds(tiles, 1), pl.ds(0, rest)]
            acc[1, pl.ds(start, count), pl.ds(0, rest)] = tail

    chunk = 32
    whole = rows // chunk

    def times_body(r, carry):
        times(pl.multiple_of(r * chunk, chunk), chunk)
        return carry

    lax.fori_loop(0, whole, times_body, 0)
    if rows - whole * chunk:
        times(whole * chunk, rows - whole * chunk)
    ones = jnp.ones((8, LANES), f32)
    own = lax.dot_general(
        ones, acc[0] + acc[1], (((1,), (1,)), ((), ())), precision=precise, preferred_element_type=f32
    )
    row8 = rows_of((8, LANES))
    tile = own[:, 0:LANES]
    for part in range(1, acc.shape[1] // LANES):
        tile = jnp.where(row8 == part, own[:, part * LANES : (part + 1) * LANES], tile)
    yown[...] = tile
    yall[w] = tile

    def y_copy(k):
        return remote(yown, yall.at[w], y_send.at[k], y_recv.at[k], "wall", lax.rem(w + k, walls))

    def y_arrival(k):
        sender = lax.rem(w + walls - k, walls)
        return remote(yown, yall.at[sender], y_send.at[k], y_recv.at[k], "wall", sender)

    for k in range(1, walls):
        y_copy(k).start()

    contract(EXT, EXT // 2, 0, strided(ping), backward(2), dense(pong))
    contract(EXT, EXT // 2, 0, strided(pong), backward(1), dense(ping))

    def place_points(g, o, total):
        solved[o, 2 * g, pl.ds(0, EXT), :] = total[0:EXT]
        solved[o, 2 * g + 1, pl.ds(0, EXT), :] = total[EXT:GROUP]

    contract(EXT, EXT // 2, 0, strided(ping), backward(0), place_points)

    span_second = [
        remote(solved.at[HIGH, inner, inner, :], face_in.at[0, :, inner, :], span_send.at[2], span_recv.at[2], "span", above),
        remote(solved.at[LOW, inner, inner, :], face_in.at[1, :, inner, :], span_send.at[3], span_recv.at[3], "span", below),
    ]
    for copy in span_second:
        copy.start()
    blank4 = jnp.zeros((16 - EXT, LANES), f32)
    for t in range(PTS):
        solved[t, LOW, pl.ds(EXT, 16 - EXT), :] = blank4
        solved[t, HIGH, pl.ds(EXT, 16 - EXT), :] = blank4
    pack(solved, HIGH, LANES - EZ, 2)
    pack(solved, LOW, 0, 3)
    send_walls(1)

    flat_solved = solved.reshape(EXT * EXT * 16, LANES)

    def stream_body(g, carry):
        def at(v):
            return pl.ds(g * (GROUP * 16) + v, GROUP, stride=16)
        low = jnp.where(inside, permute(flat_solved[at(HIGH), :], upstream), 0.0)
        high = jnp.where(inside, permute(flat_solved[at(LOW), :], downstream), 0.0)
        flat_solved[at(0), :] = flat_solved[at(0), :] + low
        flat_solved[at(PTS - 1), :] = flat_solved[at(PTS - 1), :] + high
        return carry

    lax.fori_loop(0, PTS // 2, stream_body, 0)

    for k in range(1, walls):
        y_arrival(k).wait_recv()
    factor, shift = divider(rows, verts)
    known = jnp.maximum(ids, 0)
    owner = (known * factor) >> shift
    local = known - owner * rows
    wanted = owner * 8 + (local >> 7)
    column = (rows_of((LANES, width)) == (local & (LANES - 1))).astype(f32)
    table = jnp.dot(yall[...].reshape(8 * walls, LANES), column, precision=precise, preferred_element_type=f32)
    found = jnp.sum(jnp.where(rows_of((8 * walls, width)) == wanted, table, 0.0), axis=0, keepdims=True)
    tops = found[:, 2 * LANES :]
    top = (tops, turn(tops, EZ))
    for a in range(2):
        base = found[:, a * LANES : (a + 1) * LANES]
        csum[0, pl.ds(2 * a, 1), :] = base
        csum[0, pl.ds(2 * a + 1, 1), :] = jnp.where(last_line, top[a], turn(base, -EZ))
    near = csum[0]
    far = permute(near, downstream8)
    across = []
    for ab in range(4):
        begin = jnp.broadcast_to(near[ab : ab + 1], (PTS, LANES))
        end = jnp.broadcast_to(far[ab : ab + 1], (PTS, LANES))
        across.append(begin + (end - begin) * share_v)

    def lift_body(u, carry):
        share = (2.0 * u.astype(f32) + 1.0) / (2 * PTS)
        low = across[0] + (across[1] - across[0]) * share
        high = across[2] + (across[3] - across[2]) * share
        step = high - low
        for t in range(PTS):
            solved[t, u, inner, :] = solved[t, u, inner, :] + (low + step * upper(t))
        return carry

    lax.fori_loop(0, PTS, lift_body, 0)

    receive_walls(1)
    for t in range(PTS):
        for half in range(2):
            span_rows = pl.ds(8 * half, 8)
            low = jnp.where(first_line, unpack(2, t, half, 0), turn(solved[t, HIGH, span_rows, :], EZ))
            high = jnp.where(end_line, unpack(3, t, half, LANES - EZ), turn(solved[t, LOW, span_rows, :], -EZ))
            count = 8 if half == 0 else PTS - 8
            kept = pl.ds(8 * half, count)
            solved[t, 0, kept, :] = solved[t, 0, kept, :] + low[0:count]
            solved[t, PTS - 1, kept, :] = solved[t, PTS - 1, kept, :] + high[0:count]

    def out_copy(t):
        return pltpu.make_async_copy(solved.at[t, inner, inner, :], out.at[t], out_sem.at[t])

    for t in range(1, PTS - 1):
        out_copy(t).start()
    for side, layer in ((0, 0), (1, PTS - 1)):
        span_second[side].wait_recv()

        def span_body(u, carry):
            solved[layer, u, inner, :] = solved[layer, u, inner, :] + face_in[side, u, inner, :]
            return carry

        lax.fori_loop(0, PTS, span_body, 0)
        out_copy(layer).start()

    for copy in span_first + span_second:
        copy.wait_send()
    finish_walls(0)
    finish_walls(1)
    for k in range(1, walls):
        x_copy(k).wait_send()
        y_copy(k).wait_send()
    for t in range(PTS):
        out_copy(t).wait()


def solution(mesh):
    spans, walls = mesh.shape["span"], mesh.shape["wall"]

    def per_device(residual, eig_values, eig_vectors, corner_map, stream_links, coarse_inverse):
        rows, verts = coarse_inverse.shape[1:]
        held = -(-verts // LANES)
        held = -(-held // 8) * 8
        padded = -(-rows // LANES) * LANES
        vmem = lambda *shape: pltpu.VMEM(shape, f32)
        dma = lambda count: pltpu.SemaphoreType.DMA((count,))
        return pl.pallas_call(
            functools.partial(kernel, spans, walls, verts),
            out_shape=jax.ShapeDtypeStruct(residual.shape, f32),
            in_specs=[pl.BlockSpec(memory_space=pl.ANY)] * 6,
            out_specs=pl.BlockSpec(memory_space=pl.ANY),
            scratch_shapes=[
                vmem(PTS, EXT, 16, LANES),
                vmem(2, EXT, 16, LANES),
                vmem(EXT * SLAB, LANES),
                vmem(EXT * SLAB, LANES),
                vmem(EXT, EXT, 16, LANES),
                vmem(*eig_vectors.shape),
                vmem(*eig_values.shape),
                pltpu.VMEM(corner_map.shape, jnp.int32),
                pltpu.SMEM(stream_links.shape, jnp.int32),
                vmem(rows, verts),
                vmem(2, padded, LANES),
                vmem(2, 8, LANES),
                vmem(held, LANES),
                vmem(walls, held, LANES),
                vmem(8, LANES),
                vmem(walls, 8, LANES),
                vmem(4, 24, LANES),
                vmem(4, 24, LANES),
                vmem(2, PTS, 16, LANES),
                dma(6), dma(PTS), dma(4), dma(4), dma(4), dma(4),
                dma(walls), dma(walls), dma(walls), dma(walls),
            ],
            compiler_params=pltpu.CompilerParams(
                collective_id=0, has_side_effects=True, vmem_limit_bytes=40 * 2**20
            ),
        )(residual, eig_values, eig_vectors, corner_map, stream_links, coarse_inverse)

    return jax.shard_map(
        per_device,
        mesh=mesh,
        in_specs=(
            P(None, None, None, ("span", "wall")),
            P(None, None, ("span", "wall")),
            P(None, None, None, ("span", "wall")),
            P(None, ("span", "wall")),
            P(),
            P("span", "wall", None),
        ),
        out_specs=P(None, None, None, ("span", "wall")),
        check_vma=False,
    )
```

time: 263 us -> 26.4 us (0.10); the launches traced: 259 us -> 26.3 us
  blocking collectives: 137 us -> 0 us
  local copies, waits for them, and re-layouts: 63.7 us -> 3.54 us
  starting transfers between devices: 24.1 us -> 0 us
  Pallas kernels: 0 us -> 22.7 us
  other arithmetic: 22.2 us -> 0 us
  matrix products: 10.3 us -> 0 us
    unnamed x1 -> x0, blocking collectives: 69.7 us -> none
    psum x1 -> x0, blocking collectives: 66.9 us -> none  [coarse_total(): return lax.psum(vector, 'wall')]
    ppermute x8 -> x0, starting transfers between devices: 24.1 us -> none  [the longest x4 18.8 us: padded(): after = lax.ppermute(first, axis, down)]
    pallas_call x0 -> x1, Pallas kernels: none -> 22.7 us  [per_device(): pl.pallas_call(functools.partial(kernel, spans, walls, verts), out_shape=...]
    slice x22 -> x0, local copies, waits for them, and re-layouts: 14.5 us -> none  [the longest x4 2.71 us: padded(): last = lax.slice_in_dim(array, length - width, length, axis=dim)]
    gather x5 -> x0, local copies, waits for them, and re-layouts: 10.6 us -> none  [the longest x1 6.14 us: per_device(): at_corners = coarse_sol[corner_map].reshape(2, 2, 2, elements)]
    dot_general x7 -> x0, matrix products: 10.3 us -> none  [the longest x1 6.15 us: per_device(): own_rows = jnp.dot(row_block, summed, precision=precise)]
    unnamed x209 -> x12, local copies, waits for them, and re-layouts: 10.7 us -> 3.54 us
  transfers between devices with their start and end apart: 8 -> 0, of which waited for: 0 -> 0; matrix products, arithmetic and copies ran while one was open for 27% -> 0% of each run, Pallas kernels for 0% -> 0%
where the time goes in v1:
time: 26.4 us; the launch traced here: 26.3 us
  Pallas kernels  22.7 us (86%)
  local copies, waits for them, and re-layouts  3.54 us (13%)
    pallas_call x1, Pallas kernels, per_device(): pl.pallas_call(functools.partial(kernel, spans, walls, verts), out_shape=...  22.7 us
    unnamed x12, local copies, waits for them, and re-layouts  3.54 us

profile of v1, /device:TPU:8, one launch (start us, length us, event | category | flops | bytes accessed | tf_op | source)
XLA Modules:
  0.0 26.3 jit_solution(13487588076827889253)
XLA Ops:
  0.0 0.0 copy-start.4
  0.0 0.0 copy-start.3
  0.0 0.0 copy-start.1
  0.0 0.0 copy-start.2
  0.0 0.0 copy-start
  0.0 2.6 %copy.7.inv_in = f32[1,258,4128]{2,1,0:T(8,128)S(1)} copy(f32[1,258,4128]{2,0,1:T(1,128)} %param.11) | data formatting | bytes 8520192 | tf_op args[5]
  2.7 0.0 copy-done.4
  2.7 0.0 copy-done.3
  2.7 0.0 copy-done.1
  2.7 0.0 copy-done.2
  2.7 0.0 copy-done
  2.7 22.7 %shard_map.64 = f32[10,10,10,128]{3,2,1,0:T(8,128)S(1)} custom-call(f32[10,10,10,128]{3,2,1,0:T(8,128)S(1)} %copy-done, f32[3,12,128]{2,1,0:T(8,128)S(1)} %copy-done.2, f32[3,12,12,128]{3,2,1,0:T(8,128)S(1)} %copy-done.1, s32[8,128]{1,0:T(8,128)S(1)} %copy-done.3, s32[2,16]{1,0:T(2,128)S(1)} %copy-done.4, f32[1,258,4128]{2,1,0:T(8,128)S(1)} %copy.7.inv_in), custom_call_target="tpu_custom_call" | custom-call | tf_op jit(solution)/shard_map/pallas_call | solution.py:477
  25.4 0.9 %copy.9 = f32[10,10,10,128]{3,2,1,0:T(8,128)} copy(f32[10,10,10,128]{3,2,1,0:T(8,128)S(1)} %shard_map.64) | data formatting | bytes 1024000
Async XLA Ops:
  0.0 2.7 %copy-start.4 = (s32[2,16]{1,0:T(2,128)S(1)}, s32[2,16]{1,0:T(2,128)}, u32[]{:S(2)}) copy-start(s32[2,16]{1,0:T(2,128)} %link_in.1) | copy-start | bytes 388
  0.0 2.7 %copy-start.3 = (s32[8,128]{1,0:T(8,128)S(1)}, s32[8,128]{1,0:T(8,128)}, u32[]{:S(2)}) copy-start(s32[8,128]{1,0:T(8,128)} %map_in.1) | copy-start | bytes 12292
  0.0 2.7 %copy-start.1 = (f32[3,12,12,128]{3,2,1,0:T(8,128)S(1)}, f32[3,12,12,128]{3,2,1,0:T(8,128)}, u32[]{:S(2)}) copy-start(f32[3,12,12,128]{3,2,1,0:T(8,128)} %vec_in.1) | copy-start | bytes 663556
  0.0 2.7 %copy-start.2 = (f32[3,12,128]{2,1,0:T(8,128)S(1)}, f32[3,12,128]{2,1,0:T(8,128)}, u32[]{:S(2)}) copy-start(f32[3,12,128]{2,1,0:T(8,128)} %val_in.1) | copy-start | bytes 55300
  0.0 2.7 %copy-start = (f32[10,10,10,128]{3,2,1,0:T(8,128)S(1)}, f32[10,10,10,128]{3,2,1,0:T(8,128)}, u32[]{:S(2)}) copy-start(f32[10,10,10,128]{3,2,1,0:T(8,128)} %res_in.1) | copy-start | bytes 1536004

commit v2 on v1

--- a/solution.py
+++ b/solution.py
@@ -40,6 +40,17 @@
     return jnp.take_along_axis(values, jnp.broadcast_to(index, values.shape), axis=1)
 
 
+def exact(values, picks, dims):
+    picks = picks.astype(jnp.bfloat16)
+    total = None
+    for _ in range(3):
+        piece = values.astype(jnp.bfloat16)
+        values = values - piece.astype(f32)
+        term = lax.dot_general(piece, picks, (dims, ((), ())), preferred_element_type=f32)
+        total = term if total is None else total + term
+    return total
+
+
 def divider(rows, top):
     for shift in range(12, 26):
         factor = -(-(1 << shift) // rows)
@@ -48,10 +59,10 @@
     raise ValueError("no divider")
 
 
-def contract(count, groups, first, load, coeff, store):
+def contract(count, groups, first, load, coeff, store, outputs=range(EXT)):
     def body(group, carry):
         pieces = load(group)
-        for o in range(EXT):
+        for o in outputs:
             total = None
             for i in range(count):
                 term = coeff(o, i) * pieces[i]
@@ -64,10 +75,10 @@
 
 def kernel(
     spans, walls, verts,
-    res_in, val_in, vec_in, map_in, link_in, inv_in, out,
-    field, faces, ping, pong, solved, vec, val, cmap, links, inv,
-    acc, csum, xown, xall, yown, yall, pack_out, pack_in, face_in,
-    local_sem, out_sem, span_send, span_recv, wall_send, wall_recv, x_send, x_recv, y_send, y_recv,
+    res_in, val_in, vec_in, map_in, link_in, inv_in, out, corners_out,
+    field, faces, wall_face, ping, pong, face_ping, face_pong, wall_ping, wall_pong, part, mixed, solved,
+    vec, val, cmap, links, inv, acc, csum, xown, xall, yown, yall, pack_out, pack_in, face_in,
+    local_sem, out_sem, span_send, span_recv, wall_send, wall_recv, x_send, x_recv, y_send, y_recv, meet,
 ):
     s = lax.axis_index("span")
     w = lax.axis_index("wall")
@@ -81,18 +92,44 @@
     load_links = pltpu.make_async_copy(link_in, links, local_sem.at[2])
     load_vec = pltpu.make_async_copy(vec_in, vec, local_sem.at[3])
     load_val = pltpu.make_async_copy(val_in, val, local_sem.at[4])
-    load_inv = pltpu.make_async_copy(inv_in.at[0], inv, local_sem.at[5])
-    for copy in (load_field, load_map, load_links, load_vec, load_val, load_inv):
+    load_inv = pltpu.make_async_copy(inv_in.at[:, 0, :], inv, local_sem.at[5])
+    for copy in (load_links, load_map, load_field, load_vec, load_val):
         copy.start()
 
-    barrier = pltpu.get_barrier_semaphore()
-    for k in range(1, walls):
-        pl.semaphore_signal(barrier, inc=1, device_id={"wall": lax.rem(w + k, walls)})
+    across_count = 4 if walls == 16 else 1
+    along_count = walls // across_count
+    row, column = lax.div(w, across_count), lax.rem(w, across_count)
+
+    def partner(k, sign):
+        down, right = k // across_count, k % across_count
+        if sign < 0:
+            down, right = along_count - down, across_count - right
+        return lax.rem(row + down, along_count) * across_count + lax.rem(column + right, across_count)
+
+    def hops(k):
+        down, right = k // across_count, k % across_count
+        return min(down, along_count - down) + min(right, across_count - right)
+
+    partners = sorted(range(1, walls), key=lambda k: -hops(k))
+
     above = lax.rem(s + 1, spans)
     below = lax.rem(s + spans - 1, spans)
-    for peer in (above, below):
-        pl.semaphore_signal(barrier, inc=1, device_id={"span": peer})
-    pl.semaphore_wait(barrier, walls + 1)
+    even = lax.rem(s, 2) == 0
+    hears_above = jnp.logical_or(even, s == spans - 1)
+    hears_below = jnp.logical_and(even, s > 0)
+    speaks_above = jnp.logical_not(hears_above)
+    speaks_below = jnp.logical_not(hears_below)
+    barrier = pltpu.get_barrier_semaphore()
+    for k in partners:
+        pl.semaphore_signal(barrier, inc=1, device_id={"wall": partner(k, 1)})
+
+    @pl.when(speaks_above)
+    def _():
+        pl.semaphore_signal(barrier, inc=1, device_id={"span": above})
+
+    @pl.when(speaks_below)
+    def _():
+        pl.semaphore_signal(barrier, inc=1, device_id={"span": below})
 
     def remote(src, dst, send, recv, axis, peer):
         return pltpu.make_async_remote_copy(
@@ -103,9 +140,6 @@
         remote(res_in.at[PTS - 1], faces.at[0, inner, inner, :], span_send.at[0], span_recv.at[0], "span", above),
         remote(res_in.at[0], faces.at[1, inner, inner, :], span_send.at[1], span_recv.at[1], "span", below),
     ]
-    for copy in span_first:
-        copy.start()
-
     def wall_copies(turn_index):
         base = 2 * turn_index
         up = remote(pack_out.at[base], pack_in.at[base], wall_send.at[base], wall_recv.at[base],
@@ -190,7 +224,19 @@
     load_field.wait()
     pack(field, PTS - 1, LANES - EZ, 0)
     pack(field, 0, 0, 1)
+    greeted = walls - 1 + hears_above.astype(jnp.int32) + hears_below.astype(jnp.int32)
+    pl.semaphore_wait(barrier, greeted)
     send_walls(0)
+
+    @pl.when(hears_above)
+    def _():
+        pl.semaphore_signal(meet.at[1], inc=1, device_id={"span": above})
+        span_first[0].start()
+
+    @pl.when(hears_below)
+    def _():
+        pl.semaphore_signal(meet.at[0], inc=1, device_id={"span": below})
+        span_first[1].start()
 
     def corner_body(u, sums):
         total = None
@@ -235,38 +281,52 @@
     ], axis=1)
     width = 3 * LANES
     held = xown.shape[0]
+    used = pl.ds(0, tiles + (1 if rest else 0))
     spread = jnp.where(rows_of((held, width)) == (ids >> 7), values, 0.0)
     onehot = (rows_of((LANES, width)) == (ids & (LANES - 1))).astype(f32)
-    xown[...] = lax.dot_general(
-        spread, onehot, (((1,), (1,)), ((), ())), precision=precise, preferred_element_type=f32
-    )
+    xown[...] = exact(spread, onehot, ((1,), (1,)))
 
     def x_copy(k):
-        return remote(xown, xall.at[k], x_send.at[k], x_recv.at[k], "wall", lax.rem(w + k, walls))
-
-    for k in range(1, walls):
+        return remote(xown.at[used], xall.at[k, used], x_send.at[k], x_recv.at[k], "wall", partner(k, 1))
+
+    for k in partners:
         x_copy(k).start()
 
-    receive_walls(0)
+    load_inv.start()
+
     first_line = lane < EZ
     end_line = lane >= LANES - EZ
-    for t in range(PTS):
+
+    def wall_body(t, carry):
         for half in range(2):
             span_rows = pl.ds(8 * half, 8)
             low = turn(field[t, PTS - 1, span_rows, :], EZ)
-            field[t, LOW, span_rows, :] = jnp.where(first_line, unpack(0, t, half, 0), low)
+            field[t, LOW, span_rows, :] = jnp.where(first_line, 0.0, low)
             high = turn(field[t, 0, span_rows, :], -EZ)
-            field[t, HIGH, span_rows, :] = jnp.where(end_line, unpack(1, t, half, LANES - EZ), high)
+            field[t, HIGH, span_rows, :] = jnp.where(end_line, 0.0, high)
+        return carry
+
+    lax.fori_loop(0, PTS, wall_body, 0)
+
+    @pl.when(speaks_above)
+    def _():
+        pl.semaphore_wait(meet.at[0], 1)
+        span_first[0].start()
+
+    @pl.when(jnp.logical_not(even))
+    def _():
+        pl.semaphore_wait(meet.at[1], 1)
+        span_first[1].start()
 
     def vector(direction, point, mode):
         return jnp.broadcast_to(vec[direction, point, pl.ds(mode, 1), :], (GROUP, LANES))
 
-    def strided(ref):
-        return lambda g: [ref[pl.ds(g * (GROUP * EXT) + i, GROUP, stride=EXT), :] for i in range(EXT)]
-
-    def dense(ref):
+    def strided(ref, count=EXT):
+        return lambda g: [ref[pl.ds(g * (GROUP * count) + i, GROUP, stride=count), :] for i in range(count)]
+
+    def dense(ref, length=SLAB):
         def put(g, o, total):
-            ref[pl.ds(pl.multiple_of(o * SLAB + g * GROUP, 8), GROUP), :] = total
+            ref[pl.ds(pl.multiple_of(o * length + g * GROUP, 8), GROUP), :] = total
         return put
 
     load_vec.wait()
@@ -286,91 +346,123 @@
 
     forward = lambda d: lambda o, i: vector(d, POINT[i], o)
     backward = lambda d: lambda o, i: vector(d, POINT[o], i)
-    contract(EXT, PTS // 2, 0, load_first, forward(2), dense(ping))
+    short = EXT * PTS
+    contract(EXT, PTS // 2, 0, load_first, forward(2), dense(ping, short))
+    contract(EXT, PTS // 2, 0, strided(ping), forward(1), dense(pong, short))
+    contract(PTS, EXT // 2, 0, strided(pong, PTS), forward(0), dense(part))
+
+    @pl.when(s == 0)
+    def _():
+        pl.semaphore_wait(meet.at[1], 1)
+        span_first[1].start()
+
+    def y_copy(k):
+        return remote(yown, yall.at[w], y_send.at[k], y_recv.at[k], "wall", partner(k, 1))
+
+    def y_arrival(k):
+        sender = partner(k, -1)
+        return remote(yown, yall.at[sender], y_send.at[k], y_recv.at[k], "wall", sender)
+
+    def coarse_solve():
+        load_inv.wait()
+        for k in range(1, walls):
+            x_copy(k).wait_recv()
+        total_x = xown[...]
+        for k in range(1, walls):
+            total_x = total_x + xall[k]
+        xall[0] = total_x
+
+        def times(start, count):
+            total = None
+            for c in range(tiles):
+                term = inv[pl.ds(start, count), pl.ds(c * LANES, LANES)] * xall[0, pl.ds(c, 1), :]
+                total = term if total is None else total + term
+            acc[0, pl.ds(start, count), :] = total
+            if rest:
+                tail = inv[pl.ds(start, count), pl.ds(tiles * LANES, rest)] * xall[0, pl.ds(tiles, 1), pl.ds(0, rest)]
+                acc[1, pl.ds(start, count), pl.ds(0, rest)] = tail
+
+        chunk = 32
+        whole = rows // chunk
+
+        def times_body(r, carry):
+            times(pl.multiple_of(r * chunk, chunk), chunk)
+            return carry
+
+        lax.fori_loop(0, whole, times_body, 0)
+        if rows - whole * chunk:
+            times(whole * chunk, rows - whole * chunk)
+        ones = jnp.ones((8, LANES), f32)
+        own = lax.dot_general(
+            ones, acc[0] + acc[1], (((1,), (1,)), ((), ())), precision=precise, preferred_element_type=f32
+        )
+        row8 = rows_of((8, LANES))
+        tile = own[:, 0:LANES]
+        for part in range(1, acc.shape[1] // LANES):
+            tile = jnp.where(row8 == part, own[:, part * LANES : (part + 1) * LANES], tile)
+        yown[...] = tile
+        yall[w] = tile
+
+        for k in partners:
+            y_copy(k).start()
+
+    pl.when(s == 0)(coarse_solve)
+
+    receive_walls(0)
+    for t in range(PTS):
+        for half in range(2):
+            kept = jnp.where(end_line, unpack(1, t, half, LANES - EZ), 0.0)
+            wall_face[t, pl.ds(8 * half, 8), :] = jnp.where(first_line, unpack(0, t, half, 0), kept)
+    flat_wall = wall_face.reshape(PTS * 16, LANES)
+    pieces = [flat_wall[pl.ds(v, PTS, stride=16), :] for v in range(PTS)]
+    for o in range(EXT):
+        total = None
+        for v in range(PTS):
+            term = vec[2, POINT[v], pl.ds(o, 1), :] * pieces[v]
+            total = term if total is None else total + term
+        wall_ping[pl.ds(16 * o, PTS), :] = total
+    pieces = [wall_ping[pl.ds(t, EXT, stride=16), :] for t in range(PTS)]
+    for o in range(EXT):
+        total = None
+        for t in range(PTS):
+            term = vec[0, POINT[t], pl.ds(o, 1), :] * pieces[t]
+            total = term if total is None else total + term
+        wall_pong[pl.ds(GROUP * o, EXT), :] = total
+        wall_pong[pl.ds(GROUP * o + EXT, EXT), :] = total
     for copy in span_first:
         copy.wait_recv()
-    contract(PTS, EXT // 2, PTS // 2, load_faces, forward(2), dense(ping))
-    contract(EXT, EXT // 2, 0, strided(ping), forward(1), dense(pong))
+    contract(PTS, 1, 0, load_faces, forward(2), dense(face_ping, GROUP))
+    contract(EXT, 1, 0, strided(face_ping), forward(1), dense(face_pong, GROUP))
 
     second_half = rows_of((GROUP, LANES)) >= EXT
+    left_lanes = lanes_of((GROUP, LANES)) < LANES // 2
     third = jnp.concatenate([val[2], val[2]], axis=0)
 
-    def scaled(ref):
-        put = dense(ref)
-
-        def divide(g, o, total):
-            firsts = jnp.broadcast_to(val[1, pl.ds(2 * g, 1), :], (GROUP, LANES))
-            seconds = jnp.broadcast_to(val[1, pl.ds(2 * g + 1, 1), :], (GROUP, LANES))
-            both = jnp.where(second_half, seconds, firsts) + third
-            put(g, o, total / (jnp.broadcast_to(val[0, pl.ds(o, 1), :], (GROUP, LANES)) + both))
-        return divide
-
-    contract(EXT, EXT // 2, 0, strided(pong), forward(0), scaled(ping))
-
-    load_inv.wait()
-    for k in range(1, walls):
-        x_copy(k).wait_recv()
-    total_x = xown[...]
-    for k in range(1, walls):
-        total_x = total_x + xall[k]
-    xall[0] = total_x
-
-    def times(start, count):
-        total = None
-        for c in range(tiles):
-            term = inv[pl.ds(start, count), pl.ds(c * LANES, LANES)] * xall[0, pl.ds(c, 1), :]
-            total = term if total is None else total + term
-        acc[0, pl.ds(start, count), :] = total
-        if rest:
-            tail = inv[pl.ds(start, count), pl.ds(tiles * LANES, rest)] * xall[0, pl.ds(tiles, 1), pl.ds(0, rest)]
-            acc[1, pl.ds(start, count), pl.ds(0, rest)] = tail
-
-    chunk = 32
-    whole = rows // chunk
-
-    def times_body(r, carry):
-        times(pl.multiple_of(r * chunk, chunk), chunk)
+    def halves(pick, g):
+        return jnp.where(second_half, pick(2 * g + 1), pick(2 * g))
+
+    def finish_body(g, carry):
+        low = face_pong[pl.ds(g * (2 * GROUP), GROUP, stride=2), :]
+        high = face_pong[pl.ds(g * (2 * GROUP) + 1, GROUP, stride=2), :]
+        scale = halves(lambda b: jnp.where(left_lanes, vector(1, POINT[LOW], b), vector(1, POINT[HIGH], b)), g)
+        both = third + halves(lambda b: jnp.broadcast_to(val[1, pl.ds(b, 1), :], (GROUP, LANES)), g)
+        for a in range(EXT):
+            spot = pl.ds(pl.multiple_of(a * SLAB + g * GROUP, 8), GROUP)
+            total = part[spot, :] + scale * wall_pong[pl.ds(GROUP * a, GROUP), :]
+            total = total + vector(0, POINT[LOW], a) * low + vector(0, POINT[HIGH], a) * high
+            part[spot, :] = total / (jnp.broadcast_to(val[0, pl.ds(a, 1), :], (GROUP, LANES)) + both)
         return carry
 
-    lax.fori_loop(0, whole, times_body, 0)
-    if rows - whole * chunk:
-        times(whole * chunk, rows - whole * chunk)
-    ones = jnp.ones((8, LANES), f32)
-    own = lax.dot_general(
-        ones, acc[0] + acc[1], (((1,), (1,)), ((), ())), precision=precise, preferred_element_type=f32
-    )
-    row8 = rows_of((8, LANES))
-    tile = own[:, 0:LANES]
-    for part in range(1, acc.shape[1] // LANES):
-        tile = jnp.where(row8 == part, own[:, part * LANES : (part + 1) * LANES], tile)
-    yown[...] = tile
-    yall[w] = tile
-
-    def y_copy(k):
-        return remote(yown, yall.at[w], y_send.at[k], y_recv.at[k], "wall", lax.rem(w + k, walls))
-
-    def y_arrival(k):
-        sender = lax.rem(w + walls - k, walls)
-        return remote(yown, yall.at[sender], y_send.at[k], y_recv.at[k], "wall", sender)
-
-    for k in range(1, walls):
-        y_copy(k).start()
-
-    contract(EXT, EXT // 2, 0, strided(ping), backward(2), dense(pong))
-    contract(EXT, EXT // 2, 0, strided(pong), backward(1), dense(ping))
+    lax.fori_loop(0, EXT // 2, finish_body, 0)
+    contract(EXT, EXT // 2, 0, strided(part), backward(2), dense(mixed))
+    contract(EXT, EXT // 2, 0, strided(mixed), backward(1), dense(part))
 
     def place_points(g, o, total):
         solved[o, 2 * g, pl.ds(0, EXT), :] = total[0:EXT]
         solved[o, 2 * g + 1, pl.ds(0, EXT), :] = total[EXT:GROUP]
 
-    contract(EXT, EXT // 2, 0, strided(ping), backward(0), place_points)
-
-    span_second = [
-        remote(solved.at[HIGH, inner, inner, :], face_in.at[0, :, inner, :], span_send.at[2], span_recv.at[2], "span", above),
-        remote(solved.at[LOW, inner, inner, :], face_in.at[1, :, inner, :], span_send.at[3], span_recv.at[3], "span", below),
-    ]
-    for copy in span_second:
-        copy.start()
+    last = EXT // 2 - 1
+    contract(EXT, last + 1, last, strided(part), backward(0), place_points)
     blank4 = jnp.zeros((16 - EXT, LANES), f32)
     for t in range(PTS):
         solved[t, LOW, pl.ds(EXT, 16 - EXT), :] = blank4
@@ -378,6 +470,18 @@
     pack(solved, HIGH, LANES - EZ, 2)
     pack(solved, LOW, 0, 3)
     send_walls(1)
+
+    contract(EXT, last, 0, strided(part), backward(0), place_points, (LOW, HIGH))
+
+    span_second = [
+        remote(solved.at[HIGH, inner, inner, :], face_in.at[0, :, inner, :], span_send.at[2], span_recv.at[2], "span", above),
+        remote(solved.at[LOW, inner, inner, :], face_in.at[1, :, inner, :], span_send.at[3], span_recv.at[3], "span", below),
+    ]
+    for copy in span_second:
+        copy.start()
+    contract(EXT, last, 0, strided(part), backward(0), place_points, range(PTS))
+
+    pl.when(s > 0)(coarse_solve)
 
     flat_solved = solved.reshape(EXT * EXT * 16, LANES)
 
@@ -391,41 +495,6 @@
         return carry
 
     lax.fori_loop(0, PTS // 2, stream_body, 0)
-
-    for k in range(1, walls):
-        y_arrival(k).wait_recv()
-    factor, shift = divider(rows, verts)
-    known = jnp.maximum(ids, 0)
-    owner = (known * factor) >> shift
-    local = known - owner * rows
-    wanted = owner * 8 + (local >> 7)
-    column = (rows_of((LANES, width)) == (local & (LANES - 1))).astype(f32)
-    table = jnp.dot(yall[...].reshape(8 * walls, LANES), column, precision=precise, preferred_element_type=f32)
-    found = jnp.sum(jnp.where(rows_of((8 * walls, width)) == wanted, table, 0.0), axis=0, keepdims=True)
-    tops = found[:, 2 * LANES :]
-    top = (tops, turn(tops, EZ))
-    for a in range(2):
-        base = found[:, a * LANES : (a + 1) * LANES]
-        csum[0, pl.ds(2 * a, 1), :] = base
-        csum[0, pl.ds(2 * a + 1, 1), :] = jnp.where(last_line, top[a], turn(base, -EZ))
-    near = csum[0]
-    far = permute(near, downstream8)
-    across = []
-    for ab in range(4):
-        begin = jnp.broadcast_to(near[ab : ab + 1], (PTS, LANES))
-        end = jnp.broadcast_to(far[ab : ab + 1], (PTS, LANES))
-        across.append(begin + (end - begin) * share_v)
-
-    def lift_body(u, carry):
-        share = (2.0 * u.astype(f32) + 1.0) / (2 * PTS)
-        low = across[0] + (across[1] - across[0]) * share
-        high = across[2] + (across[3] - across[2]) * share
-        step = high - low
-        for t in range(PTS):
-            solved[t, u, inner, :] = solved[t, u, inner, :] + (low + step * upper(t))
-        return carry
-
-    lax.fori_loop(0, PTS, lift_body, 0)
 
     receive_walls(1)
     for t in range(PTS):
@@ -453,6 +522,29 @@
         lax.fori_loop(0, PTS, span_body, 0)
         out_copy(layer).start()
 
+    factor, shift = divider(rows, verts)
+    known = jnp.maximum(ids, 0)
+    owner = (known * factor) >> shift
+    local = known - owner * rows
+    wanted = owner * 8 + (local >> 7)
+    column_picks = (rows_of((LANES, width)) == (local & (LANES - 1))).astype(f32)
+    picks = column_picks.astype(jnp.bfloat16)
+    for k in range(1, walls):
+        y_arrival(k).wait_recv()
+    table = exact(yall[...].reshape(8 * walls, LANES), picks, ((1,), (0,)))
+    found = jnp.sum(jnp.where(rows_of((8 * walls, width)) == wanted, table, 0.0), axis=0, keepdims=True)
+    tops = found[:, 2 * LANES :]
+    top = (tops, turn(tops, EZ))
+    for a in range(2):
+        base = found[:, a * LANES : (a + 1) * LANES]
+        csum[0, pl.ds(2 * a, 1), :] = base
+        csum[0, pl.ds(2 * a + 1, 1), :] = jnp.where(last_line, top[a], turn(base, -EZ))
+    near = csum[0]
+    far = permute(near, downstream8)
+    csum[1] = far
+    corner_copy = pltpu.make_async_copy(csum, corners_out, local_sem.at[5])
+    corner_copy.start()
+
     for copy in span_first + span_second:
         copy.wait_send()
     finish_walls(0)
@@ -462,6 +554,35 @@
         y_copy(k).wait_send()
     for t in range(PTS):
         out_copy(t).wait()
+    corner_copy.wait()
+
+
+def lift(base, corners, out, held, near, low_lift, step_lift, in_sem, out_sem, near_sem):
+    near_copy = pltpu.make_async_copy(corners, near, near_sem)
+    near_copy.start()
+    loads = [pltpu.make_async_copy(base.at[t], held.at[t], in_sem.at[t]) for t in range(PTS)]
+    stores = [pltpu.make_async_copy(held.at[t], out.at[t], out_sem.at[t]) for t in range(PTS)]
+    for copy in loads:
+        copy.start()
+    near_copy.wait()
+    share = (2.0 * rows_of((PTS, LANES)).astype(f32) + 1.0) / (2 * PTS)
+    across = []
+    for ab in range(4):
+        begin = jnp.broadcast_to(near[0, pl.ds(ab, 1), :], (PTS, LANES))
+        end = jnp.broadcast_to(near[1, pl.ds(ab, 1), :], (PTS, LANES))
+        across.append(begin + (end - begin) * share)
+    for u in range(PTS):
+        low = across[0] + (across[1] - across[0]) * upper(u)
+        high = across[2] + (across[3] - across[2]) * upper(u)
+        low_lift[u] = low
+        step_lift[u] = high - low
+    for t in range(PTS):
+        loads[t].wait()
+        for u in range(PTS):
+            held[t, u] = held[t, u] + (low_lift[u] + step_lift[u] * upper(t))
+        stores[t].start()
+    for copy in stores:
+        copy.wait()
 
 
 def solution(mesh):
@@ -474,14 +595,21 @@
         padded = -(-rows // LANES) * LANES
         vmem = lambda *shape: pltpu.VMEM(shape, f32)
         dma = lambda count: pltpu.SemaphoreType.DMA((count,))
-        return pl.pallas_call(
+        base, corners = pl.pallas_call(
             functools.partial(kernel, spans, walls, verts),
-            out_shape=jax.ShapeDtypeStruct(residual.shape, f32),
-            in_specs=[pl.BlockSpec(memory_space=pl.ANY)] * 6,
-            out_specs=pl.BlockSpec(memory_space=pl.ANY),
+            out_shape=[jax.ShapeDtypeStruct(residual.shape, f32), jax.ShapeDtypeStruct((2, 8, LANES), f32)],
+            in_specs=[pl.BlockSpec(memory_space=pltpu.HBM)] * 6,
+            out_specs=[pl.BlockSpec(memory_space=pl.ANY)] * 2,
             scratch_shapes=[
                 vmem(PTS, EXT, 16, LANES),
                 vmem(2, EXT, 16, LANES),
+                vmem(PTS, 16, LANES),
+                vmem(EXT * EXT * PTS, LANES),
+                vmem(EXT * EXT * PTS, LANES),
+                vmem(EXT * GROUP, LANES),
+                vmem(EXT * GROUP, LANES),
+                vmem(EXT * 16, LANES),
+                vmem(EXT * GROUP, LANES),
                 vmem(EXT * SLAB, LANES),
                 vmem(EXT * SLAB, LANES),
                 vmem(EXT, EXT, 16, LANES),
@@ -501,11 +629,26 @@
                 vmem(2, PTS, 16, LANES),
                 dma(6), dma(PTS), dma(4), dma(4), dma(4), dma(4),
                 dma(walls), dma(walls), dma(walls), dma(walls),
+                pltpu.SemaphoreType.REGULAR((2,)),
             ],
             compiler_params=pltpu.CompilerParams(
-                collective_id=0, has_side_effects=True, vmem_limit_bytes=40 * 2**20
+                collective_id=0, has_side_effects=True, vmem_limit_bytes=60 * 2**20
             ),
-        )(residual, eig_values, eig_vectors, corner_map, stream_links, coarse_inverse)
+        )(residual, eig_values, eig_vectors, corner_map, stream_links, jnp.transpose(coarse_inverse, (1, 0, 2)))
+        return pl.pallas_call(
+            lift,
+            out_shape=jax.ShapeDtypeStruct(residual.shape, f32),
+            in_specs=[pl.BlockSpec(memory_space=pltpu.HBM)] * 2,
+            out_specs=pl.BlockSpec(memory_space=pl.ANY),
+            scratch_shapes=[
+                vmem(PTS, PTS, PTS, LANES),
+                vmem(2, 8, LANES),
+                vmem(PTS, PTS, LANES),
+                vmem(PTS, PTS, LANES),
+                dma(PTS), dma(PTS), pltpu.SemaphoreType.DMA,
+            ],
+            compiler_params=pltpu.CompilerParams(vmem_limit_bytes=60 * 2**20),
+        )(base, corners)
 
     return jax.shard_map(
         per_device,

time: 26.4 us -> 23.3 us (0.88)
  local copies, waits for them, and re-layouts: 3.54 us -> 0 us
  Pallas kernels: 22.7 us -> 23.1 us
    unnamed x12 -> x0, local copies, waits for them, and re-layouts: 3.54 us -> none
    pallas_call x0 -> x1, Pallas kernels: none -> 1.94 us  [per_device(): pl.pallas_call(lift, out_shape=jax.ShapeDtypeStruct(residual.shape, f32),...]
    pallas_call x1, Pallas kernels: 22.7 us -> 21.2 us  [per_device(): pl.pallas_call(functools.partial(kernel, spans, walls, verts), out_shape=...]
where the time goes in v2:
time: 23.3 us; the launch traced here: 23.1 us
  Pallas kernels  23.1 us (99%)
    pallas_call x1, Pallas kernels, per_device(): pl.pallas_call(functools.partial(kernel, spans, walls, verts), out_shape=...  21.2 us
    pallas_call x1, Pallas kernels, per_device(): pl.pallas_call(lift, out_shape=jax.ShapeDtypeStruct(residual.shape, f32),...  1.94 us

profile of v2, /device:TPU:8, one launch (start us, length us, event | category | flops | bytes accessed | tf_op | source)
XLA Modules:
  0.0 23.1 jit_solution(3317714651626430373)
XLA Ops:
  0.0 21.2 %shard_map.64 = (f32[10,10,10,128]{3,2,1,0:T(8,128)}, f32[2,8,128]{2,1,0:T(8,128)}) custom-call(f32[10,10,10,128]{3,2,1,0:T(8,128)} %res_in.1, f32[3,12,128]{2,1,0:T(8,128)} %val_in.1, f32[3,12,12,128]{3,2,1,0:T(8,128)} %vec_in.1, s32[8,128]{1,0:T(8,128)} %map_in.1, s32[2,16]{1,0:T(2,128)} %link_in.1, f32[258,1,4128]{2,1,0:T(1,128)} %bitcast.1), custom_call_target="tpu_custom_call" | custom-call | tf_op jit(solution)/shard_map/pallas_call | solution.py:598
  21.2 1.9 %shard_map.65 = f32[10,10,10,128]{3,2,1,0:T(8,128)} custom-call(f32[10,10,10,128]{3,2,1,0:T(8,128)} %get-tuple-element.7.base, f32[2,8,128]{2,1,0:T(8,128)} %get-tuple-element.8.corners), custom_call_target="tpu_custom_call" | custom-call | tf_op jit(solution)/shard_map/pallas_call | solution.py:638

commit v3 on v2

--- a/solution.py
+++ b/solution.py
@@ -40,13 +40,14 @@
     return jnp.take_along_axis(values, jnp.broadcast_to(index, values.shape), axis=1)
 
 
-def exact(values, picks, dims):
+def exact(values, picks, dims, swapped=False):
     picks = picks.astype(jnp.bfloat16)
     total = None
     for _ in range(3):
         piece = values.astype(jnp.bfloat16)
         values = values - piece.astype(f32)
-        term = lax.dot_general(piece, picks, (dims, ((), ())), preferred_element_type=f32)
+        pair = (picks, piece) if swapped else (piece, picks)
+        term = lax.dot_general(*pair, (dims, ((), ())), preferred_element_type=f32)
         total = term if total is None else total + term
     return total
 
@@ -75,9 +76,10 @@
 
 def kernel(
     spans, walls, verts,
-    res_in, val_in, vec_in, map_in, link_in, inv_in, out, corners_out,
-    field, faces, wall_face, ping, pong, face_ping, face_pong, wall_ping, wall_pong, part, mixed, solved,
-    vec, val, cmap, links, inv, acc, csum, xown, xall, yown, yall, pack_out, pack_in, face_in,
+    res_in, val_in, vec_in, map_in, link_in, inv_in, out, faces_out, walls_out, yall, index_out,
+    field, faces, wall_face, ping, pong, face_ping, face_pong, wall_ping, wall_pong, part, mixed, divisor,
+    side_first, side_second, side_third, wall_one, wall_two, wall_three, solved,
+    vec, val, cmap, links, inv, acc, csum, xown, xall, yown, index, pack_out, pack_in,
     local_sem, out_sem, span_send, span_recv, wall_send, wall_recv, x_send, x_recv, y_send, y_recv, meet,
 ):
     s = lax.axis_index("span")
@@ -119,6 +121,7 @@
     hears_below = jnp.logical_and(even, s > 0)
     speaks_above = jnp.logical_not(hears_above)
     speaks_below = jnp.logical_not(hears_below)
+    early = row + column < 3
     barrier = pltpu.get_barrier_semaphore()
     for k in partners:
         pl.semaphore_signal(barrier, inc=1, device_id={"wall": partner(k, 1)})
@@ -142,9 +145,10 @@
     ]
     def wall_copies(turn_index):
         base = 2 * turn_index
-        up = remote(pack_out.at[base], pack_in.at[base], wall_send.at[base], wall_recv.at[base],
+        landing = walls_out if turn_index else pack_in
+        up = remote(pack_out.at[base], landing.at[0], wall_send.at[base], wall_recv.at[base],
                     "wall", lax.rem(w + 1, walls))
-        down = remote(pack_out.at[base + 1], pack_in.at[base + 1], wall_send.at[base + 1], wall_recv.at[base + 1],
+        down = remote(pack_out.at[base + 1], landing.at[1], wall_send.at[base + 1], wall_recv.at[base + 1],
                       "wall", lax.rem(w + walls - 1, walls))
         return up, down
 
@@ -169,12 +173,12 @@
     lane = lanes_of((8, LANES))
     slot_of = lane // EZ
 
-    def pack(source, layer, lane_from, dest):
+    def pack(source, lane_from, dest):
         parts = [None] * 3
         for t in range(PTS):
             for half in range(2):
                 slot = 2 * t + half
-                piece = source[t, layer, pl.ds(8 * half, 8), :]
+                piece = source(t, half)
                 place = slot % 8
                 moved = turn(piece, EZ * place - lane_from)
                 held = parts[slot // 8]
@@ -182,20 +186,18 @@
         for index, part in enumerate(parts):
             pack_out[dest, pl.ds(8 * index, 8), :] = part
 
-    def unpack(buffer, t, half, lane_to):
-        slot = 2 * t + half
-        part = pack_in[buffer, pl.ds(8 * (slot // 8), 8), :]
-        return turn(part, lane_to - EZ * (slot % 8))
+    def no_neighbour(side):
+        return pltpu.make_async_copy(pack_in.at[side], walls_out.at[side], out_sem.at[PTS + side])
 
     @pl.when(jnp.logical_not(has_down))
     def _():
-        for turn_index in range(2):
-            pack_in[2 * turn_index] = jnp.zeros(pack_in.shape[1:], f32)
+        pack_in[0] = jnp.zeros(pack_in.shape[1:], f32)
+        no_neighbour(0).start()
 
     @pl.when(jnp.logical_not(has_up))
     def _():
-        for turn_index in range(2):
-            pack_in[2 * turn_index + 1] = jnp.zeros(pack_in.shape[1:], f32)
+        pack_in[1] = jnp.zeros(pack_in.shape[1:], f32)
+        no_neighbour(1).start()
 
     blank = jnp.zeros((16 - PTS, LANES), f32)
     for t in range(PTS):
@@ -222,8 +224,64 @@
     downstream = jnp.concatenate([downstream8] * 3, axis=0)
 
     load_field.wait()
-    pack(field, PTS - 1, LANES - EZ, 0)
-    pack(field, 0, 0, 1)
+    pack(lambda t, half: field[t, PTS - 1, pl.ds(8 * half, 8), :], LANES - EZ, 0)
+    pack(lambda t, half: field[t, 0, pl.ds(8 * half, 8), :], 0, 1)
+    used = pl.ds(0, tiles + (1 if rest else 0))
+    width = 3 * LANES
+    index_copy = pltpu.make_async_copy(index, index_out, local_sem.at[6])
+
+    def vertex_sums():
+        def corner_body(u, sums):
+            total = None
+            weighted = None
+            for t in range(PTS):
+                piece = field[t, u, inner, :]
+                term = piece * upper(t)
+                total = piece if total is None else total + piece
+                weighted = term if weighted is None else weighted + term
+            low = total - weighted
+            share = (2.0 * u.astype(f32) + 1.0) / (2 * PTS)
+            low_up = low * share
+            high_up = weighted * share
+            return (sums[0] + (low - low_up), sums[1] + low_up,
+                    sums[2] + (weighted - high_up), sums[3] + high_up)
+
+        nothing = jnp.zeros((PTS, LANES), f32)
+        sums = lax.fori_loop(0, PTS, corner_body, (nothing,) * 4)
+        share_v = (2.0 * rows_of((PTS, LANES)).astype(f32) + 1.0) / (2 * PTS)
+        for ab in range(4):
+            upper_part = sums[ab] * share_v
+            csum[0, pl.ds(ab, 1), :] = jnp.sum(sums[ab] - upper_part, axis=0, keepdims=True)
+            csum[1, pl.ds(ab, 1), :] = jnp.sum(upper_part, axis=0, keepdims=True)
+        lines = csum[0] + permute(csum[1], upstream8)
+        moved_up = jnp.where(lane >= EZ, turn(lines, EZ), 0.0)
+        moved_down = turn(lines, -EZ)
+        lane1 = lanes_of((1, LANES))
+        last_line = lane1 >= LANES - EZ
+        second_line = lane1 >= LANES - 2 * EZ
+        values = jnp.concatenate([
+            lines[0:1] + moved_up[1:2],
+            lines[2:3] + moved_up[3:4],
+            jnp.where(last_line, lines[1:2], jnp.where(second_line, moved_down[3:4], 0.0)),
+        ], axis=1)
+
+        load_map.wait()
+        moved_map = turn(cmap[...], -EZ)
+        ids = jnp.concatenate([
+            cmap[0:1, :],
+            cmap[4:5, :],
+            jnp.where(last_line, cmap[2:3, :], jnp.where(second_line, moved_map[6:7], -1)),
+        ], axis=1)
+        index[pl.ds(0, 8), :] = jnp.broadcast_to(ids, (8, width))
+        index[pl.ds(8, 8), :] = jnp.concatenate([downstream8] * 3, axis=1)
+        index_copy.start()
+        held = xown.shape[0]
+        spread = jnp.where(rows_of((held, width)) == (ids >> 7), values, 0.0)
+        onehot = (rows_of((LANES, width)) == (ids & (LANES - 1))).astype(f32)
+        xown[...] = exact(spread, onehot, ((1,), (1,)))
+
+    pl.when(early)(vertex_sums)
+
     greeted = walls - 1 + hears_above.astype(jnp.int32) + hears_below.astype(jnp.int32)
     pl.semaphore_wait(barrier, greeted)
     send_walls(0)
@@ -231,67 +289,20 @@
     @pl.when(hears_above)
     def _():
         pl.semaphore_signal(meet.at[1], inc=1, device_id={"span": above})
-        span_first[0].start()
 
     @pl.when(hears_below)
     def _():
         pl.semaphore_signal(meet.at[0], inc=1, device_id={"span": below})
-        span_first[1].start()
-
-    def corner_body(u, sums):
-        total = None
-        weighted = None
-        for t in range(PTS):
-            piece = field[t, u, inner, :]
-            term = piece * upper(t)
-            total = piece if total is None else total + piece
-            weighted = term if weighted is None else weighted + term
-        low = total - weighted
-        share = (2.0 * u.astype(f32) + 1.0) / (2 * PTS)
-        low_up = low * share
-        high_up = weighted * share
-        return (sums[0] + (low - low_up), sums[1] + low_up,
-                sums[2] + (weighted - high_up), sums[3] + high_up)
-
-    nothing = jnp.zeros((PTS, LANES), f32)
-    sums = lax.fori_loop(0, PTS, corner_body, (nothing,) * 4)
-    share_v = (2.0 * rows_of((PTS, LANES)).astype(f32) + 1.0) / (2 * PTS)
-    for ab in range(4):
-        upper_part = sums[ab] * share_v
-        csum[0, pl.ds(ab, 1), :] = jnp.sum(sums[ab] - upper_part, axis=0, keepdims=True)
-        csum[1, pl.ds(ab, 1), :] = jnp.sum(upper_part, axis=0, keepdims=True)
-    lines = csum[0] + permute(csum[1], upstream8)
-    moved_up = jnp.where(lane >= EZ, turn(lines, EZ), 0.0)
-    moved_down = turn(lines, -EZ)
-    lane1 = lanes_of((1, LANES))
-    last_line = lane1 >= LANES - EZ
-    second_line = lane1 >= LANES - 2 * EZ
-    values = jnp.concatenate([
-        lines[0:1] + moved_up[1:2],
-        lines[2:3] + moved_up[3:4],
-        jnp.where(last_line, lines[1:2], jnp.where(second_line, moved_down[3:4], 0.0)),
-    ], axis=1)
-
-    load_map.wait()
-    moved_map = turn(cmap[...], -EZ)
-    ids = jnp.concatenate([
-        cmap[0:1, :],
-        cmap[4:5, :],
-        jnp.where(last_line, cmap[2:3, :], jnp.where(second_line, moved_map[6:7], -1)),
-    ], axis=1)
-    width = 3 * LANES
-    held = xown.shape[0]
-    used = pl.ds(0, tiles + (1 if rest else 0))
-    spread = jnp.where(rows_of((held, width)) == (ids >> 7), values, 0.0)
-    onehot = (rows_of((LANES, width)) == (ids & (LANES - 1))).astype(f32)
-    xown[...] = exact(spread, onehot, ((1,), (1,)))
+
+    pl.when(jnp.logical_not(early))(vertex_sums)
 
     def x_copy(k):
         return remote(xown.at[used], xall.at[k, used], x_send.at[k], x_recv.at[k], "wall", partner(k, 1))
 
     for k in partners:
         x_copy(k).start()
-
+    pl.when(hears_above)(span_first[0].start)
+    pl.when(hears_below)(span_first[1].start)
     load_inv.start()
 
     first_line = lane < EZ
@@ -351,10 +362,28 @@
     contract(EXT, PTS // 2, 0, strided(ping), forward(1), dense(pong, short))
     contract(PTS, EXT // 2, 0, strided(pong, PTS), forward(0), dense(part))
 
+    second_half = rows_of((GROUP, LANES)) >= EXT
+    left_lanes = lanes_of((GROUP, LANES)) < LANES // 2
+    third = jnp.concatenate([val[2], val[2]], axis=0)
+
+    def halves(pick, g):
+        return jnp.where(second_half, pick(2 * g + 1), pick(2 * g))
+
+    def divisor_body(g, carry):
+        both = third + halves(lambda b: jnp.broadcast_to(val[1, pl.ds(b, 1), :], (GROUP, LANES)), g)
+        for a in range(EXT):
+            spot = pl.ds(pl.multiple_of(a * SLAB + g * GROUP, 8), GROUP)
+            divisor[spot, :] = 1.0 / (jnp.broadcast_to(val[0, pl.ds(a, 1), :], (GROUP, LANES)) + both)
+        return carry
+
+    lax.fori_loop(0, EXT // 2, divisor_body, 0)
+
     @pl.when(s == 0)
     def _():
         pl.semaphore_wait(meet.at[1], 1)
         span_first[1].start()
+
+    y_keep = pltpu.make_async_copy(yown, yall.at[w], local_sem.at[7])
 
     def y_copy(k):
         return remote(yown, yall.at[w], y_send.at[k], y_recv.at[k], "wall", partner(k, 1))
@@ -393,15 +422,13 @@
         if rows - whole * chunk:
             times(whole * chunk, rows - whole * chunk)
         ones = jnp.ones((8, LANES), f32)
-        own = lax.dot_general(
-            ones, acc[0] + acc[1], (((1,), (1,)), ((), ())), precision=precise, preferred_element_type=f32
-        )
+        own = exact(acc[0] + acc[1], ones, ((1,), (1,)), True)
         row8 = rows_of((8, LANES))
         tile = own[:, 0:LANES]
         for part in range(1, acc.shape[1] // LANES):
             tile = jnp.where(row8 == part, own[:, part * LANES : (part + 1) * LANES], tile)
         yown[...] = tile
-        yall[w] = tile
+        y_keep.start()
 
         for k in partners:
             y_copy(k).start()
@@ -411,8 +438,8 @@
     receive_walls(0)
     for t in range(PTS):
         for half in range(2):
-            kept = jnp.where(end_line, unpack(1, t, half, LANES - EZ), 0.0)
-            wall_face[t, pl.ds(8 * half, 8), :] = jnp.where(first_line, unpack(0, t, half, 0), kept)
+            kept = jnp.where(end_line, unpack(pack_in, 1, t, half, LANES - EZ), 0.0)
+            wall_face[t, pl.ds(8 * half, 8), :] = jnp.where(first_line, unpack(pack_in, 0, t, half, 0), kept)
     flat_wall = wall_face.reshape(PTS * 16, LANES)
     pieces = [flat_wall[pl.ds(v, PTS, stride=16), :] for v in range(PTS)]
     for o in range(EXT):
@@ -434,56 +461,86 @@
     contract(PTS, 1, 0, load_faces, forward(2), dense(face_ping, GROUP))
     contract(EXT, 1, 0, strided(face_ping), forward(1), dense(face_pong, GROUP))
 
-    second_half = rows_of((GROUP, LANES)) >= EXT
-    left_lanes = lanes_of((GROUP, LANES)) < LANES // 2
-    third = jnp.concatenate([val[2], val[2]], axis=0)
-
-    def halves(pick, g):
-        return jnp.where(second_half, pick(2 * g + 1), pick(2 * g))
-
     def finish_body(g, carry):
         low = face_pong[pl.ds(g * (2 * GROUP), GROUP, stride=2), :]
         high = face_pong[pl.ds(g * (2 * GROUP) + 1, GROUP, stride=2), :]
         scale = halves(lambda b: jnp.where(left_lanes, vector(1, POINT[LOW], b), vector(1, POINT[HIGH], b)), g)
-        both = third + halves(lambda b: jnp.broadcast_to(val[1, pl.ds(b, 1), :], (GROUP, LANES)), g)
         for a in range(EXT):
             spot = pl.ds(pl.multiple_of(a * SLAB + g * GROUP, 8), GROUP)
             total = part[spot, :] + scale * wall_pong[pl.ds(GROUP * a, GROUP), :]
             total = total + vector(0, POINT[LOW], a) * low + vector(0, POINT[HIGH], a) * high
-            part[spot, :] = total / (jnp.broadcast_to(val[0, pl.ds(a, 1), :], (GROUP, LANES)) + both)
+            part[spot, :] = total * divisor[spot, :]
         return carry
 
     lax.fori_loop(0, EXT // 2, finish_body, 0)
+    def contract_small(pieces, coeff, outputs, store):
+        for o in outputs:
+            total = None
+            for i in range(EXT):
+                term = coeff(o, i) * pieces[i]
+                total = term if total is None else total + term
+            store(o, total)
+
+    def entry(direction, point, mode):
+        return vec[direction, point, pl.ds(mode, 1), :]
+
+    def slabs(g):
+        return [part[pl.ds(pl.multiple_of(a * SLAB + g * GROUP, 8), GROUP), :] for a in range(EXT)]
+
+    def put_side(g, o, total):
+        side_first[pl.ds(pl.multiple_of((o - PTS) * SLAB + g * GROUP, 8), GROUP), :] = total
+
+    contract(EXT, EXT // 2, 0, slabs, backward(0), put_side, (LOW, HIGH))
+    for side in range(2):
+        def put_second(o, total):
+            side_second[pl.ds(16 * o, EXT), :] = total
+
+        def put_third(o, total):
+            side_third[side, o, pl.ds(0, EXT), :] = total
+
+        pieces = [side_first[pl.ds(side * SLAB + c, EXT, stride=EXT), :] for c in range(EXT)]
+        contract_small(pieces, lambda o, i: entry(2, POINT[o], i), range(EXT), put_second)
+        pieces = [side_second[pl.ds(b, EXT, stride=16), :] for b in range(EXT)]
+        contract_small(pieces, lambda o, i: entry(1, POINT[o], i), range(PTS), put_third)
+    span_second = [
+        remote(side_third.at[1, :, inner, :], faces_out.at[0], span_send.at[2], span_recv.at[2], "span", above),
+        remote(side_third.at[0, :, inner, :], faces_out.at[1], span_send.at[3], span_recv.at[3], "span", below),
+    ]
+    for copy in span_second:
+        copy.start()
+
+    def wall_first(a, carry):
+        pieces = [part[pl.ds(a * SLAB + b * EXT, EXT), :] for b in range(EXT)]
+
+        def put(o, total):
+            wall_one[pl.ds((o - PTS) * SLAB + a * EXT, EXT), :] = total
+
+        contract_small(pieces, lambda o, i: entry(1, POINT[o], i), (LOW, HIGH), put)
+        return carry
+
+    lax.fori_loop(0, EXT, wall_first, 0)
+    contract(EXT, 1, 0, strided(wall_one), backward(2), dense(wall_two, GROUP))
+    wall_three[pl.ds(PTS * GROUP, 16), :] = jnp.zeros((16, LANES), f32)
+    contract(EXT, 1, 0, strided(wall_two), backward(0), dense(wall_three, GROUP), range(PTS))
+
+    def wall_layer(t, half, layer):
+        return wall_three[pl.ds(t * GROUP + 16 * half + (layer - PTS), 8, stride=2), :]
+
+    pack(lambda t, half: wall_layer(t, half, HIGH), LANES - EZ, 2)
+    pack(lambda t, half: wall_layer(t, half, LOW), 0, 3)
+    send_walls(1)
+
     contract(EXT, EXT // 2, 0, strided(part), backward(2), dense(mixed))
-    contract(EXT, EXT // 2, 0, strided(mixed), backward(1), dense(part))
+    pl.when(s > 0)(coarse_solve)
+    contract(EXT, EXT // 2, 0, strided(mixed), backward(1), dense(part), range(PTS))
 
     def place_points(g, o, total):
         solved[o, 2 * g, pl.ds(0, EXT), :] = total[0:EXT]
         solved[o, 2 * g + 1, pl.ds(0, EXT), :] = total[EXT:GROUP]
 
-    last = EXT // 2 - 1
-    contract(EXT, last + 1, last, strided(part), backward(0), place_points)
-    blank4 = jnp.zeros((16 - EXT, LANES), f32)
-    for t in range(PTS):
-        solved[t, LOW, pl.ds(EXT, 16 - EXT), :] = blank4
-        solved[t, HIGH, pl.ds(EXT, 16 - EXT), :] = blank4
-    pack(solved, HIGH, LANES - EZ, 2)
-    pack(solved, LOW, 0, 3)
-    send_walls(1)
-
-    contract(EXT, last, 0, strided(part), backward(0), place_points, (LOW, HIGH))
-
-    span_second = [
-        remote(solved.at[HIGH, inner, inner, :], face_in.at[0, :, inner, :], span_send.at[2], span_recv.at[2], "span", above),
-        remote(solved.at[LOW, inner, inner, :], face_in.at[1, :, inner, :], span_send.at[3], span_recv.at[3], "span", below),
-    ]
-    for copy in span_second:
-        copy.start()
-    contract(EXT, last, 0, strided(part), backward(0), place_points, range(PTS))
-
-    pl.when(s > 0)(coarse_solve)
-
-    flat_solved = solved.reshape(EXT * EXT * 16, LANES)
+    contract(EXT, PTS // 2, 0, strided(part), backward(0), place_points, range(PTS))
+
+    flat_solved = solved.reshape(PTS * EXT * 16, LANES)
 
     def stream_body(g, carry):
         def at(v):
@@ -496,55 +553,40 @@
 
     lax.fori_loop(0, PTS // 2, stream_body, 0)
 
-    receive_walls(1)
-    for t in range(PTS):
+    def own_walls(t, carry):
         for half in range(2):
             span_rows = pl.ds(8 * half, 8)
-            low = jnp.where(first_line, unpack(2, t, half, 0), turn(solved[t, HIGH, span_rows, :], EZ))
-            high = jnp.where(end_line, unpack(3, t, half, LANES - EZ), turn(solved[t, LOW, span_rows, :], -EZ))
+            low = jnp.where(first_line, 0.0, turn(wall_layer(t, half, HIGH), EZ))
+            high = jnp.where(end_line, 0.0, turn(wall_layer(t, half, LOW), -EZ))
             count = 8 if half == 0 else PTS - 8
             kept = pl.ds(8 * half, count)
             solved[t, 0, kept, :] = solved[t, 0, kept, :] + low[0:count]
             solved[t, PTS - 1, kept, :] = solved[t, PTS - 1, kept, :] + high[0:count]
+        return carry
+
+    lax.fori_loop(0, PTS, own_walls, 0)
 
     def out_copy(t):
         return pltpu.make_async_copy(solved.at[t, inner, inner, :], out.at[t], out_sem.at[t])
 
-    for t in range(1, PTS - 1):
+    for t in range(PTS):
         out_copy(t).start()
-    for side, layer in ((0, 0), (1, PTS - 1)):
-        span_second[side].wait_recv()
-
-        def span_body(u, carry):
-            solved[layer, u, inner, :] = solved[layer, u, inner, :] + face_in[side, u, inner, :]
-            return carry
-
-        lax.fori_loop(0, PTS, span_body, 0)
-        out_copy(layer).start()
-
-    factor, shift = divider(rows, verts)
-    known = jnp.maximum(ids, 0)
-    owner = (known * factor) >> shift
-    local = known - owner * rows
-    wanted = owner * 8 + (local >> 7)
-    column_picks = (rows_of((LANES, width)) == (local & (LANES - 1))).astype(f32)
-    picks = column_picks.astype(jnp.bfloat16)
+    index_copy.wait()
+
+    @pl.when(jnp.logical_not(has_down))
+    def _():
+        no_neighbour(0).wait()
+
+    @pl.when(jnp.logical_not(has_up))
+    def _():
+        no_neighbour(1).wait()
+
+    receive_walls(1)
+    for copy in span_second:
+        copy.wait_recv()
     for k in range(1, walls):
         y_arrival(k).wait_recv()
-    table = exact(yall[...].reshape(8 * walls, LANES), picks, ((1,), (0,)))
-    found = jnp.sum(jnp.where(rows_of((8 * walls, width)) == wanted, table, 0.0), axis=0, keepdims=True)
-    tops = found[:, 2 * LANES :]
-    top = (tops, turn(tops, EZ))
-    for a in range(2):
-        base = found[:, a * LANES : (a + 1) * LANES]
-        csum[0, pl.ds(2 * a, 1), :] = base
-        csum[0, pl.ds(2 * a + 1, 1), :] = jnp.where(last_line, top[a], turn(base, -EZ))
-    near = csum[0]
-    far = permute(near, downstream8)
-    csum[1] = far
-    corner_copy = pltpu.make_async_copy(csum, corners_out, local_sem.at[5])
-    corner_copy.start()
-
+    y_keep.wait()
     for copy in span_first + span_second:
         copy.wait_send()
     finish_walls(0)
@@ -554,32 +596,84 @@
         y_copy(k).wait_send()
     for t in range(PTS):
         out_copy(t).wait()
-    corner_copy.wait()
-
-
-def lift(base, corners, out, held, near, low_lift, step_lift, in_sem, out_sem, near_sem):
-    near_copy = pltpu.make_async_copy(corners, near, near_sem)
-    near_copy.start()
+
+
+def unpack(packed, side, t, half, lane_to):
+    slot = 2 * t + half
+    part = packed[side, pl.ds(8 * (slot // 8), 8), :]
+    return turn(part, lane_to - EZ * (slot % 8))
+
+
+def lift(
+    rows, verts, base, faces, packed, values, index, out,
+    held, faces_here, packed_here, values_here, index_here, near, low_lift, step_lift, in_sem, out_sem, small_sem,
+):
+    smalls = [
+        pltpu.make_async_copy(there, here, small_sem.at[k])
+        for k, (there, here) in enumerate((
+            (index, index_here), (values, values_here), (packed, packed_here), (faces, faces_here)
+        ))
+    ]
     loads = [pltpu.make_async_copy(base.at[t], held.at[t], in_sem.at[t]) for t in range(PTS)]
     stores = [pltpu.make_async_copy(held.at[t], out.at[t], out_sem.at[t]) for t in range(PTS)]
-    for copy in loads:
+    order = tuple(range(1, PTS - 1)) + (0, PTS - 1)
+    for copy in smalls[:3] + [loads[t] for t in order[:-2]] + smalls[3:] + [loads[t] for t in order[-2:]]:
         copy.start()
-    near_copy.wait()
+    smalls[0].wait()
+    width = 3 * LANES
+    count = values_here.shape[0] * 8
+    ids = index_here[pl.ds(0, 1), :]
+    downstream8 = index_here[pl.ds(8, 8), pl.ds(0, LANES)]
+    factor, shift = divider(rows, verts)
+    known = jnp.maximum(ids, 0)
+    owner = (known * factor) >> shift
+    local = known - owner * rows
+    wanted = owner * 8 + (local >> 7)
+    picks = (rows_of((LANES, width)) == (local & (LANES - 1))).astype(f32).astype(jnp.bfloat16)
+    smalls[1].wait()
+    table = exact(values_here[...].reshape(count, LANES), picks, ((1,), (0,)))
+    found = jnp.sum(jnp.where(rows_of((count, width)) == wanted, table, 0.0), axis=0, keepdims=True)
+    last_line = lanes_of((1, LANES)) >= LANES - EZ
+    tops = found[:, 2 * LANES :]
+    top = (tops, turn(tops, EZ))
+    near[...] = jnp.zeros(near.shape, f32)
+    for a in range(2):
+        row = found[:, a * LANES : (a + 1) * LANES]
+        near[pl.ds(2 * a, 1), :] = row
+        near[pl.ds(2 * a + 1, 1), :] = jnp.where(last_line, top[a], turn(row, -EZ))
+    begins = near[...]
+    ends = permute(begins, downstream8)
     share = (2.0 * rows_of((PTS, LANES)).astype(f32) + 1.0) / (2 * PTS)
     across = []
     for ab in range(4):
-        begin = jnp.broadcast_to(near[0, pl.ds(ab, 1), :], (PTS, LANES))
-        end = jnp.broadcast_to(near[1, pl.ds(ab, 1), :], (PTS, LANES))
+        begin = jnp.broadcast_to(begins[ab : ab + 1], (PTS, LANES))
+        end = jnp.broadcast_to(ends[ab : ab + 1], (PTS, LANES))
         across.append(begin + (end - begin) * share)
     for u in range(PTS):
         low = across[0] + (across[1] - across[0]) * upper(u)
         high = across[2] + (across[3] - across[2]) * upper(u)
         low_lift[u] = low
         step_lift[u] = high - low
-    for t in range(PTS):
+    smalls[2].wait()
+    first_line = lanes_of((8, LANES)) < EZ
+    end_line = lanes_of((8, LANES)) >= LANES - EZ
+    for t in order:
         loads[t].wait()
         for u in range(PTS):
             held[t, u] = held[t, u] + (low_lift[u] + step_lift[u] * upper(t))
+        for half in range(2):
+            size = 8 if half == 0 else PTS - 8
+            kept = pl.ds(8 * half, size)
+            low = jnp.where(first_line, unpack(packed_here, 0, t, half, 0), 0.0)
+            high = jnp.where(end_line, unpack(packed_here, 1, t, half, LANES - EZ), 0.0)
+            held[t, 0, kept, :] = held[t, 0, kept, :] + low[0:size]
+            held[t, PTS - 1, kept, :] = held[t, PTS - 1, kept, :] + high[0:size]
+        if t in (0, PTS - 1):
+            side = 0 if t == 0 else 1
+            if t == 0:
+                smalls[3].wait()
+            for u in range(PTS):
+                held[t, u] = held[t, u] + faces_here[side, u]
         stores[t].start()
     for copy in stores:
         copy.wait()
@@ -595,11 +689,18 @@
         padded = -(-rows // LANES) * LANES
         vmem = lambda *shape: pltpu.VMEM(shape, f32)
         dma = lambda count: pltpu.SemaphoreType.DMA((count,))
-        base, corners = pl.pallas_call(
+        shapes = [
+            jax.ShapeDtypeStruct(residual.shape, f32),
+            jax.ShapeDtypeStruct((2, PTS, PTS, LANES), f32),
+            jax.ShapeDtypeStruct((2, 24, LANES), f32),
+            jax.ShapeDtypeStruct((walls, 8, LANES), f32),
+            jax.ShapeDtypeStruct((16, 3 * LANES), jnp.int32),
+        ]
+        parts = pl.pallas_call(
             functools.partial(kernel, spans, walls, verts),
-            out_shape=[jax.ShapeDtypeStruct(residual.shape, f32), jax.ShapeDtypeStruct((2, 8, LANES), f32)],
+            out_shape=shapes,
             in_specs=[pl.BlockSpec(memory_space=pltpu.HBM)] * 6,
-            out_specs=[pl.BlockSpec(memory_space=pl.ANY)] * 2,
+            out_specs=[pl.BlockSpec(memory_space=pl.ANY)] * 5,
             scratch_shapes=[
                 vmem(PTS, EXT, 16, LANES),
                 vmem(2, EXT, 16, LANES),
@@ -612,7 +713,14 @@
                 vmem(EXT * GROUP, LANES),
                 vmem(EXT * SLAB, LANES),
                 vmem(EXT * SLAB, LANES),
-                vmem(EXT, EXT, 16, LANES),
+                vmem(EXT * SLAB, LANES),
+                vmem(2 * SLAB, LANES),
+                vmem(EXT * 16, LANES),
+                vmem(2, PTS, 16, LANES),
+                vmem(2 * SLAB, LANES),
+                vmem(EXT * GROUP, LANES),
+                vmem(PTS * GROUP + 16, LANES),
+                vmem(PTS, EXT, 16, LANES),
                 vmem(*eig_vectors.shape),
                 vmem(*eig_values.shape),
                 pltpu.VMEM(corner_map.shape, jnp.int32),
@@ -623,11 +731,10 @@
                 vmem(held, LANES),
                 vmem(walls, held, LANES),
                 vmem(8, LANES),
-                vmem(walls, 8, LANES),
+                pltpu.VMEM((16, 3 * LANES), jnp.int32),
                 vmem(4, 24, LANES),
-                vmem(4, 24, LANES),
-                vmem(2, PTS, 16, LANES),
-                dma(6), dma(PTS), dma(4), dma(4), dma(4), dma(4),
+                vmem(2, 24, LANES),
+                dma(8), dma(PTS + 2), dma(4), dma(4), dma(4), dma(4),
                 dma(walls), dma(walls), dma(walls), dma(walls),
                 pltpu.SemaphoreType.REGULAR((2,)),
             ],
@@ -636,19 +743,23 @@
             ),
         )(residual, eig_values, eig_vectors, corner_map, stream_links, jnp.transpose(coarse_inverse, (1, 0, 2)))
         return pl.pallas_call(
-            lift,
+            functools.partial(lift, rows, verts),
             out_shape=jax.ShapeDtypeStruct(residual.shape, f32),
-            in_specs=[pl.BlockSpec(memory_space=pltpu.HBM)] * 2,
+            in_specs=[pl.BlockSpec(memory_space=pltpu.HBM)] * 5,
             out_specs=pl.BlockSpec(memory_space=pl.ANY),
             scratch_shapes=[
-                vmem(PTS, PTS, PTS, LANES),
-                vmem(2, 8, LANES),
+                vmem(*residual.shape),
+                vmem(2, PTS, PTS, LANES),
+                vmem(2, 24, LANES),
+                vmem(walls, 8, LANES),
+                pltpu.VMEM((16, 3 * LANES), jnp.int32),
+                vmem(8, LANES),
                 vmem(PTS, PTS, LANES),
                 vmem(PTS, PTS, LANES),
-                dma(PTS), dma(PTS), pltpu.SemaphoreType.DMA,
+                dma(PTS), dma(PTS), dma(4),
             ],
             compiler_params=pltpu.CompilerParams(vmem_limit_bytes=60 * 2**20),
-        )(base, corners)
+        )(*parts)
 
     return jax.shard_map(
         per_device,

time: 23.3 us -> 22.3 us (0.957)
  Pallas kernels: 23.1 us -> 22 us
    pallas_call x1, Pallas kernels: 21.2 us -> 18.9 us  [per_device(): pl.pallas_call(functools.partial(kernel, spans, walls, verts), out_shape=...]
    pallas_call x1, Pallas kernels: 1.94 us -> 3.04 us  [per_device(): pl.pallas_call(functools.partial(lift, rows, verts), out_shape=jax.ShapeD...]
where the time goes in v3:
time: 22.3 us; the launch traced here: 22 us
  Pallas kernels  22 us (99%)
    pallas_call x1, Pallas kernels, per_device(): pl.pallas_call(functools.partial(kernel, spans, walls, verts), out_shape=...  18.9 us
    pallas_call x1, Pallas kernels, per_device(): pl.pallas_call(functools.partial(lift, rows, verts), out_shape=jax.ShapeD...  3.04 us

profile of v3, /device:TPU:8, one launch (start us, length us, event | category | flops | bytes accessed | tf_op | source)
XLA Modules:
  0.0 22.0 jit_solution(17757466825455076119)
XLA Ops:
  0.0 18.9 %shard_map.64 = (f32[10,10,10,128]{3,2,1,0:T(8,128)}, f32[2,10,10,128]{3,2,1,0:T(8,128)}, f32[2,24,128]{2,1,0:T(8,128)}, f32[16,8,128]{2,1,0:T(8,128)}, s32[16,384]{1,0:T(8,128)}) custom-call(f32[10,10,10,128]{3,2,1,0:T(8,128)} %res_in.1, f32[3,12,128]{2,1,0:T(8,128)} %val_in.1, f32[3,12,12,128]{3,2,1,0:T(8,128)} %vec_in.1, s32[8,128]{1,0:T(8,128)} %map_in.1, ...), custom_call_target="tpu_custom_call" | custom-call | tf_op jit(solution)/shard_map/pallas_call | solution.py:699
  18.9 3.0 %shard_map.65 = f32[10,10,10,128]{3,2,1,0:T(8,128)} custom-call(f32[10,10,10,128]{3,2,1,0:T(8,128)} %get-tuple-element.10.base, f32[2,10,10,128]{3,2,1,0:T(8,128)} %get-tuple-element.11.faces, f32[2,24,128]{2,1,0:T(8,128)} %get-tuple-element.12.packed, f32[16,8,128]{2,1,0:T(8,128)} %get-tuple-element.13.values, s32[16,384]{1,0:T(8,128)} %get-tuple-element.14.index), custom_call_target="tpu_custom_call" | custom-call | tf_op jit(solution)/shard_map/pallas_call | solution.py:745

commit v4 on v3

--- a/solution.py
+++ b/solution.py
@@ -401,26 +401,30 @@
             total_x = total_x + xall[k]
         xall[0] = total_x
 
-        def times(start, count):
-            total = None
+        def times(start, count, ways):
+            sums = [None] * ways
             for c in range(tiles):
                 term = inv[pl.ds(start, count), pl.ds(c * LANES, LANES)] * xall[0, pl.ds(c, 1), :]
-                total = term if total is None else total + term
+                held = sums[c % ways]
+                sums[c % ways] = term if held is None else held + term
+            total = sums[0]
+            for part_sum in sums[1:]:
+                total = total + part_sum
             acc[0, pl.ds(start, count), :] = total
             if rest:
                 tail = inv[pl.ds(start, count), pl.ds(tiles * LANES, rest)] * xall[0, pl.ds(tiles, 1), pl.ds(0, rest)]
                 acc[1, pl.ds(start, count), pl.ds(0, rest)] = tail
 
-        chunk = 32
+        chunk = 64
         whole = rows // chunk
 
         def times_body(r, carry):
-            times(pl.multiple_of(r * chunk, chunk), chunk)
+            times(pl.multiple_of(r * chunk, chunk), chunk, 2)
             return carry
 
         lax.fori_loop(0, whole, times_body, 0)
         if rows - whole * chunk:
-            times(whole * chunk, rows - whole * chunk)
+            times(whole * chunk, rows - whole * chunk, 8)
         ones = jnp.ones((8, LANES), f32)
         own = exact(acc[0] + acc[1], ones, ((1,), (1,)), True)
         row8 = rows_of((8, LANES))
@@ -606,7 +610,7 @@
 
 def lift(
     rows, verts, base, faces, packed, values, index, out,
-    held, faces_here, packed_here, values_here, index_here, near, low_lift, step_lift, in_sem, out_sem, small_sem,
+    held, faces_here, packed_here, values_here, index_here, near, low_lift, step_lift, wall_add, in_sem, out_sem, small_sem,
 ):
     smalls = [
         pltpu.make_async_copy(there, here, small_sem.at[k])
@@ -630,6 +634,14 @@
     local = known - owner * rows
     wanted = owner * 8 + (local >> 7)
     picks = (rows_of((LANES, width)) == (local & (LANES - 1))).astype(f32).astype(jnp.bfloat16)
+    smalls[2].wait()
+    first_line = lanes_of((8, LANES)) < EZ
+    end_line = lanes_of((8, LANES)) >= LANES - EZ
+    for t in range(PTS):
+        for half in range(2):
+            kept = pl.ds(8 * half, 8)
+            wall_add[0, t, kept, :] = jnp.where(first_line, unpack(packed_here, 0, t, half, 0), 0.0)
+            wall_add[1, t, kept, :] = jnp.where(end_line, unpack(packed_here, 1, t, half, LANES - EZ), 0.0)
     smalls[1].wait()
     table = exact(values_here[...].reshape(count, LANES), picks, ((1,), (0,)))
     found = jnp.sum(jnp.where(rows_of((count, width)) == wanted, table, 0.0), axis=0, keepdims=True)
@@ -654,20 +666,12 @@
         high = across[2] + (across[3] - across[2]) * upper(u)
         low_lift[u] = low
         step_lift[u] = high - low
-    smalls[2].wait()
-    first_line = lanes_of((8, LANES)) < EZ
-    end_line = lanes_of((8, LANES)) >= LANES - EZ
     for t in order:
         loads[t].wait()
         for u in range(PTS):
             held[t, u] = held[t, u] + (low_lift[u] + step_lift[u] * upper(t))
-        for half in range(2):
-            size = 8 if half == 0 else PTS - 8
-            kept = pl.ds(8 * half, size)
-            low = jnp.where(first_line, unpack(packed_here, 0, t, half, 0), 0.0)
-            high = jnp.where(end_line, unpack(packed_here, 1, t, half, LANES - EZ), 0.0)
-            held[t, 0, kept, :] = held[t, 0, kept, :] + low[0:size]
-            held[t, PTS - 1, kept, :] = held[t, PTS - 1, kept, :] + high[0:size]
+        held[t, 0] = held[t, 0] + wall_add[0, t, pl.ds(0, PTS), :]
+        held[t, PTS - 1] = held[t, PTS - 1] + wall_add[1, t, pl.ds(0, PTS), :]
         if t in (0, PTS - 1):
             side = 0 if t == 0 else 1
             if t == 0:
@@ -756,6 +760,7 @@
                 vmem(8, LANES),
                 vmem(PTS, PTS, LANES),
                 vmem(PTS, PTS, LANES),
+                vmem(2, PTS, 16, LANES),
                 dma(PTS), dma(PTS), dma(4),
             ],
             compiler_params=pltpu.CompilerParams(vmem_limit_bytes=60 * 2**20),

time: 22.3 us -> 21.7 us (0.973)
  Pallas kernels: 22 us -> 21.5 us
    pallas_call x1, Pallas kernels: 3.04 us -> 2.6 us  [per_device(): pl.pallas_call(functools.partial(lift, rows, verts), out_shape=jax.ShapeD...]
where the time goes in v4:
time: 21.7 us; the launch traced here: 21.6 us
  Pallas kernels  21.5 us (99%)
    pallas_call x1, Pallas kernels, per_device(): pl.pallas_call(functools.partial(kernel, spans, walls, verts), out_shape=...  18.9 us
    pallas_call x1, Pallas kernels, per_device(): pl.pallas_call(functools.partial(lift, rows, verts), out_shape=jax.ShapeD...  2.6 us

profile of v4, /device:TPU:8, one launch (start us, length us, event | category | flops | bytes accessed | tf_op | source)
XLA Modules:
  0.0 21.6 jit_solution(14117138632909578540)
XLA Ops:
  0.0 18.9 %shard_map.64 = (f32[10,10,10,128]{3,2,1,0:T(8,128)}, f32[2,10,10,128]{3,2,1,0:T(8,128)}, f32[2,24,128]{2,1,0:T(8,128)}, f32[16,8,128]{2,1,0:T(8,128)}, s32[16,384]{1,0:T(8,128)}) custom-call(f32[10,10,10,128]{3,2,1,0:T(8,128)} %res_in.1, f32[3,12,128]{2,1,0:T(8,128)} %val_in.1, f32[3,12,12,128]{3,2,1,0:T(8,128)} %vec_in.1, s32[8,128]{1,0:T(8,128)} %map_in.1, ...), custom_call_target="tpu_custom_call" | custom-call | tf_op jit(solution)/shard_map/pallas_call | solution.py:703
  18.9 2.6 %shard_map.65 = f32[10,10,10,128]{3,2,1,0:T(8,128)} custom-call(f32[10,10,10,128]{3,2,1,0:T(8,128)} %get-tuple-element.10.base, f32[2,10,10,128]{3,2,1,0:T(8,128)} %get-tuple-element.11.faces, f32[2,24,128]{2,1,0:T(8,128)} %get-tuple-element.12.packed, f32[16,8,128]{2,1,0:T(8,128)} %get-tuple-element.13.values, s32[16,384]{1,0:T(8,128)} %get-tuple-element.14.index), custom_call_target="tpu_custom_call" | custom-call | tf_op jit(solution)/shard_map/pallas_call | solution.py:749

commit v5 on v4

--- a/solution.py
+++ b/solution.py
@@ -121,7 +121,7 @@
     hears_below = jnp.logical_and(even, s > 0)
     speaks_above = jnp.logical_not(hears_above)
     speaks_below = jnp.logical_not(hears_below)
-    early = row + column < 3
+    early = jnp.logical_or(row + column < 3, s < spans - 1)
     barrier = pltpu.get_barrier_semaphore()
     for k in partners:
         pl.semaphore_signal(barrier, inc=1, device_id={"wall": partner(k, 1)})

time: 21.7 us -> 21.7 us (level)
  no operation moved by 1% of the time
where the time goes in v5:
time: 21.7 us; the launch traced here: 21.6 us
  Pallas kernels  21.5 us (99%)
    pallas_call x1, Pallas kernels, per_device(): pl.pallas_call(functools.partial(kernel, spans, walls, verts), out_shape=...  18.9 us
    pallas_call x1, Pallas kernels, per_device(): pl.pallas_call(functools.partial(lift, rows, verts), out_shape=jax.ShapeD...  2.6 us

profile of v5, /device:TPU:8, one launch (start us, length us, event | category | flops | bytes accessed | tf_op | source)
XLA Modules:
  0.0 21.6 jit_solution(8385557046047932554)
XLA Ops:
  0.0 18.9 %shard_map.64 = (f32[10,10,10,128]{3,2,1,0:T(8,128)}, f32[2,10,10,128]{3,2,1,0:T(8,128)}, f32[2,24,128]{2,1,0:T(8,128)}, f32[16,8,128]{2,1,0:T(8,128)}, s32[16,384]{1,0:T(8,128)}) custom-call(f32[10,10,10,128]{3,2,1,0:T(8,128)} %res_in.1, f32[3,12,128]{2,1,0:T(8,128)} %val_in.1, f32[3,12,12,128]{3,2,1,0:T(8,128)} %vec_in.1, s32[8,128]{1,0:T(8,128)} %map_in.1, ...), custom_call_target="tpu_custom_call" | custom-call | tf_op jit(solution)/shard_map/pallas_call | solution.py:703
  18.9 2.6 %shard_map.65 = f32[10,10,10,128]{3,2,1,0:T(8,128)} custom-call(f32[10,10,10,128]{3,2,1,0:T(8,128)} %get-tuple-element.10.base, f32[2,10,10,128]{3,2,1,0:T(8,128)} %get-tuple-element.11.faces, f32[2,24,128]{2,1,0:T(8,128)} %get-tuple-element.12.packed, f32[16,8,128]{2,1,0:T(8,128)} %get-tuple-element.13.values, s32[16,384]{1,0:T(8,128)} %get-tuple-element.14.index), custom_call_target="tpu_custom_call" | custom-call | tf_op jit(solution)/shard_map/pallas_call | solution.py:749
